TPU v7x, 128 devices: a whole 4x4x4 slice. The times are simulated.
128 devices in a mesh: dev: 128 (over z, y, x, core).
Axes of the slice: x: 4, y: 4, z: 4, core: 2. Of those that a mesh axis runs over, the one named last changes fastest.
Arguments:
- params: float32 [59, 524288], P(None, 'dev'), as said below
- adam_m: float32 [59, 524288], P(None, 'dev'), may hold values from -3 to 3
- adam_v: float32 [59, 524288], P(None, 'dev'), may hold values from 1e-05 to 0.001
- target: float32 [3, 131072], P(None, 'dev'), may hold values from 0 to 1
- req_rows: int32 [128, 5120], P('dev'), may hold values from 0 to 4095, as said below
- tile_list: int32 [128, 5120], P('dev'), may hold values from 0 to 5119
- tile_len: int32 [512], P('dev'), may hold values from 1 to 1280, 409600 in all
- tile_order: int32 [512, 1280], P('dev'), may hold values from 0 to 1279, as said below
- tile_pos: int32 [512], P('dev'), may hold values from 0 to 511, as said below
- bg_ids: int32 [128], replicated, may hold values from 0 to 524287
Outputs:
- new_params: float32 [59, 524288], P(None, 'dev')
- new_m: float32 [59, 524288], P(None, 'dev')
- new_v: float32 [59, 524288], P(None, 'dev')
Inputs may be any that keep to these rules, and one draw needn't show every extreme that they name: `params`: device o owns region o mod 64 (tiles 2 * 4 (o mod 64) onward, in row-major order) in depth layer o // 64: its Gaussians' centers project into that region, row 2 (depth) lies in 2 to 4 in layer 0 and in 4 to 6 in layer 1; row 6 (quaternion w) lies in 0.5 to 1.5. `req_rows`: within one window's 512 slots of a device the rows are distinct. `tile_order`: each row is a permutation that orders the tile's entries by increasing depth of their Gaussians. `tile_pos`: a permutation; device d renders 4 of the 8 tiles of region d mod 64.
All inputs are finite; a program needn't handle non-finite values. No bound on the sum of `tile_len` on one device may be relied on, other than what follows from the above.
Results may differ from a plain program's by a relative error of at most 0.0003.
Values sent between devices are 32-bit elements; how exact they have to be, the bound alone decides.
A program may use at most 128 MiB of HBM per device.

v0:
```python
import functools

import jax
import jax.numpy as jnp
from jax import lax
from jax.experimental import pallas as pl
from jax.experimental.pallas import tpu as pltpu
from jax.sharding import PartitionSpec as P

TILES_X = 32
NEAR = 10
FOCAL = 512.0
BIAS_ONE = 1.0 - 0.9**10
BIAS_TWO = 1.0 - 0.999**10
MESH = pl.DeviceIdType.MESH
F32 = jnp.float32
BF16 = jnp.bfloat16
LANES = 128
INNER = 16
SPLAT = 9


def harmonics(dir_x, dir_y, dir_z):
    sq_x = dir_x * dir_x
    sq_y = dir_y * dir_y
    sq_z = dir_z * dir_z
    return [
        0.28209479177387814 + 0.0 * dir_x,
        -0.4886025119029199 * dir_y,
        0.4886025119029199 * dir_z,
        -0.4886025119029199 * dir_x,
        1.0925484305920792 * dir_x * dir_y,
        -1.0925484305920792 * dir_y * dir_z,
        0.31539156525252005 * (2.0 * sq_z - sq_x - sq_y),
        -1.0925484305920792 * dir_x * dir_z,
        0.5462742152960396 * (sq_x - sq_y),
        -0.5900435899266435 * dir_y * (3.0 * sq_x - sq_y),
        2.890611442640554 * dir_x * dir_y * dir_z,
        -0.4570457994644658 * dir_y * (4.0 * sq_z - sq_x - sq_y),
        0.3731763325901154 * dir_z * (2.0 * sq_z - 3.0 * sq_x - 3.0 * sq_y),
        -0.4570457994644658 * dir_x * (4.0 * sq_z - sq_x - sq_y),
        1.445305721320277 * dir_z * (sq_x - sq_y),
        -0.5900435899266435 * dir_x * (sq_x - 3.0 * sq_y),
    ]


def geometry(rows, center_y):
    pos_x, pos_y, depth = (rows[0], rows[1], rows[2])
    stretches = (jnp.exp(rows[3]), jnp.exp(rows[4]), jnp.exp(rows[5]))
    quat_norm = jnp.sqrt(
        rows[6] * rows[6] + rows[7] * rows[7] + rows[8] * rows[8] + rows[9] * rows[9]
    )
    inv_norm = 1.0 / quat_norm
    quat_w = rows[6] * inv_norm
    quat_x = rows[7] * inv_norm
    quat_y = rows[8] * inv_norm
    quat_z = rows[9] * inv_norm
    rotation = (
        (
            1.0 - 2.0 * (quat_y * quat_y + quat_z * quat_z),
            2.0 * (quat_x * quat_y - quat_w * quat_z),
            2.0 * (quat_x * quat_z + quat_w * quat_y),
        ),
        (
            2.0 * (quat_x * quat_y + quat_w * quat_z),
            1.0 - 2.0 * (quat_x * quat_x + quat_z * quat_z),
            2.0 * (quat_y * quat_z - quat_w * quat_x),
        ),
        (
            2.0 * (quat_x * quat_z - quat_w * quat_y),
            2.0 * (quat_y * quat_z + quat_w * quat_x),
            1.0 - 2.0 * (quat_x * quat_x + quat_y * quat_y),
        ),
    )
    inv_depth = 1.0 / depth
    focal_z = FOCAL * inv_depth
    slope_x = pos_x * inv_depth
    slope_y = pos_y * inv_depth
    cov_a = 0.3
    cov_b = 0.0
    cov_c = 0.3
    for column in range(3):
        axis_x = rotation[0][column] * stretches[column]
        axis_y = rotation[1][column] * stretches[column]
        axis_z = rotation[2][column] * stretches[column]
        image_u = focal_z * (axis_x - slope_x * axis_z)
        image_v = focal_z * (axis_y - slope_y * axis_z)
        cov_a = cov_a + image_u * image_u
        cov_b = cov_b + image_u * image_v
        cov_c = cov_c + image_v * image_v
    inv_determ = 1.0 / (cov_a * cov_c - cov_b * cov_b)
    center_u = FOCAL * slope_x + 8.0 * TILES_X
    center_v = FOCAL * slope_y + center_y
    inv_distance = 1.0 / jnp.sqrt(pos_x * pos_x + pos_y * pos_y + depth * depth)
    basis = harmonics(pos_x * inv_distance, pos_y * inv_distance, depth * inv_distance)
    conic = [cov_c * inv_determ, -cov_b * inv_determ, cov_a * inv_determ]
    return [center_u, center_v] + conic + basis


def lane_gather(source, index):
    numbers = lax.GatherDimensionNumbers(
        offset_dims=(),
        collapsed_slice_dims=(1,),
        start_index_map=(1,),
        operand_batching_dims=(0,),
        start_indices_batching_dims=(0,),
    )
    return lax.gather(
        source,
        index[..., None],
        numbers,
        (1, 1),
        mode=lax.GatherScatterMode.PROMISE_IN_BOUNDS,
    )


def wide(row, rows=8):
    return jnp.broadcast_to(row, (rows, row.shape[-1]))


def pieces_of(value):
    first = value.astype(BF16)
    return first, (value - first.astype(F32)).astype(BF16)


def project_kernel(center_y, params, bg_ids, splats, back):
    step = pl.program_id(0)
    chunk = params.shape[1]
    rows = [params[i : i + 1, :] for i in range(11)]
    made = geometry(rows, center_y)
    opacity = jax.nn.sigmoid(rows[10])
    colors = []
    for c in range(3):
        total = made[5] * params[11 + c : 12 + c, :]
        for k in range(1, 16):
            total = total + made[5 + k] * params[11 + 3 * k + c : 12 + 3 * k + c, :]
        colors.append(total + 0.5)
    for i, row in enumerate(made[:5] + [opacity] + colors):
        splats[i : i + 1, :] = row
    splats[SPLAT:16, :] = jnp.zeros((16 - SPLAT, chunk), F32)
    me = lax.axis_index("dev")
    g_local = chunk * pl.num_programs(0)

    @pl.when(step == 0)
    def _():
        back[...] = jnp.zeros_like(back)

    local = wide(bg_ids[...] - (me * g_local + step * chunk))
    high = jnp.right_shift(local, 7)
    low = jnp.bitwise_and(local, LANES - 1)
    for half in range(2):
        total = back[half * 8 : half * 8 + 8, :]
        for c in range(chunk // LANES):
            found = lane_gather(splats[half * 8 : half * 8 + 8, c * LANES : (c + 1) * LANES], low)
            total = jnp.where(high == c, found, total)
        back[half * 8 : half * 8 + 8, :] = total


def project_local(params, bg_ids, center_y):
    count, g_local = params.shape
    chunk = 512
    return pl.pallas_call(
        functools.partial(project_kernel, center_y),
        grid=(g_local // chunk,),
        out_shape=(
            jax.ShapeDtypeStruct((16, g_local), F32),
            jax.ShapeDtypeStruct((16, LANES), F32),
        ),
        in_specs=[
            pl.BlockSpec((count, chunk), lambda i: (0, i)),
            pl.BlockSpec((1, LANES), lambda i: (0, 0)),
        ],
        out_specs=(
            pl.BlockSpec((16, chunk), lambda i: (0, i)),
            pl.BlockSpec((16, LANES), lambda i: (0, 0)),
        ),
        name="project_local",
    )(params, bg_ids)


def offsets_of(devices):
    lines = [0, 1, -1, 4, -4]
    return [(lines[w % 5] + w // 5 * (devices // 2)) % devices for w in range(NEAR)]


def exchange(devices, direction, block_of, given, taken, send_sem, recv_sem, local_sem):
    me = lax.axis_index("dev")
    copies = []
    for w, offset in enumerate(offsets_of(devices)):
        if offset == 0:
            copies.append(pltpu.make_async_copy(block_of(given, w), block_of(taken, w), local_sem))
            continue
        copies.append(
            pltpu.make_async_remote_copy(
                src_ref=block_of(given, w),
                dst_ref=block_of(taken, w),
                send_sem=send_sem.at[w],
                recv_sem=recv_sem.at[w],
                device_id=(lax.rem(me + (offset * direction) % devices, devices),),
                device_id_type=MESH,
            )
        )
    return copies


def inner_partner(me, k):
    return me // INNER * INNER + lax.rem(lax.rem(me, INNER) + k, INNER)


def outer_partner(devices, me, k):
    return lax.rem(me + INNER * k, devices)


def spread(count, partner, given, taken, send_sem, recv_sem, base):
    me = lax.axis_index("dev")
    return [
        pltpu.make_async_remote_copy(
            src_ref=given,
            dst_ref=taken.at[k],
            send_sem=send_sem.at[base + k],
            recv_sem=recv_sem.at[base + k],
            device_id=(partner(me, k),),
            device_id_type=MESH,
        )
        for k in range(1, count)
    ]


def greet(devices, inner, outer):
    me = lax.axis_index("dev")
    partners = [lax.rem(me + offset, devices) for offset in offsets_of(devices) if offset]
    if inner:
        partners += [inner_partner(me, k) for k in range(1, INNER)]
    if outer:
        partners += [outer_partner(devices, me, k) for k in range(1, devices // INNER)]
    barrier = pltpu.get_barrier_semaphore()
    for partner in partners:
        pl.semaphore_signal(barrier, inc=1, device_id=(partner,), device_id_type=MESH)
    pl.semaphore_wait(barrier, len(partners))


def request_kernel(devices, req, back, wanted, gathered, send_sem, recv_sem, local_sem):
    cap = req.shape[1] // NEAR
    greet(devices, True, False)
    block = lambda ref, w: ref.at[:, pl.ds(w * cap, cap)]
    copies = exchange(devices, 1, block, req, wanted, send_sem, recv_sem, local_sem.at[0])
    copies += spread(INNER, inner_partner, back, gathered, send_sem, recv_sem, NEAR)
    copies.append(pltpu.make_async_copy(back, gathered.at[0], local_sem.at[1]))
    for copy in copies:
        copy.start()
    for copy in copies:
        copy.wait()


def supply_kernel(devices, sent, back, arrived, gathered, send_sem, recv_sem, local_sem):
    greet(devices, False, True)
    block = lambda ref, w: ref.at[w]
    copies = exchange(devices, -1, block, sent, arrived, send_sem, recv_sem, local_sem.at[0])
    partner = functools.partial(outer_partner, devices)
    copies += spread(devices // INNER, partner, back, gathered, send_sem, recv_sem, NEAR)
    copies.append(pltpu.make_async_copy(back, gathered.at[0], local_sem.at[1]))
    for copy in copies:
        copy.start()
    for copy in copies:
        copy.wait()


def return_kernel(
    devices, grads, back, returned, gathered, held, total, send_sem, recv_sem, local_sem
):
    greet(devices, True, True)
    block = lambda ref, w: ref.at[w]
    inner = spread(INNER, inner_partner, back, held, send_sem, recv_sem, NEAR)
    copies = exchange(devices, 1, block, grads, returned, send_sem, recv_sem, local_sem.at[0])
    for copy in inner + copies:
        copy.start()
    for copy in inner:
        copy.wait()
    summed = back[...]
    for k in range(1, INNER):
        summed = summed + held[k]
    total[...] = summed
    partner = functools.partial(outer_partner, devices)
    outer = spread(devices // INNER, partner, total, gathered, send_sem, recv_sem, NEAR + INNER)
    outer.append(pltpu.make_async_copy(total, gathered.at[0], local_sem.at[1]))
    for copy in outer:
        copy.start()
    for copy in outer + copies:
        copy.wait()


def communicate(kernel, ident, devices, main, back, groups, scratch, semaphores, back_space):
    spec = pl.BlockSpec(memory_space=pl.ANY)
    return pl.pallas_call(
        functools.partial(kernel, devices),
        out_shape=(
            jax.ShapeDtypeStruct(main.shape, main.dtype),
            jax.ShapeDtypeStruct((groups,) + back.shape, F32),
        ),
        in_specs=[spec, pl.BlockSpec(memory_space=back_space)],
        out_specs=(spec, spec),
        scratch_shapes=scratch
        + [
            pltpu.SemaphoreType.DMA((semaphores,)),
            pltpu.SemaphoreType.DMA((semaphores,)),
            pltpu.SemaphoreType.DMA((2,)),
        ],
        compiler_params=pltpu.CompilerParams(collective_id=ident, has_side_effects=True),
        name=kernel.__name__,
    )(main, back)


def owner_gather_kernel(splats, wanted, gathered, sent, back, index):
    for r in range(wanted.shape[1] // LANES):
        index[r : r + 1, :] = wanted[:, r * LANES : (r + 1) * LANES]
    chunks = splats.shape[1] // LANES

    @pl.loop(0, index.shape[0] // 8)
    def _(i):
        rows = index[pl.ds(pl.multiple_of(i * 8, 8), 8), :]
        high = jnp.right_shift(rows, 7)
        low = jnp.bitwise_and(rows, LANES - 1)
        totals = [jnp.zeros((8, LANES), F32) for _ in range(SPLAT)]
        for c in range(chunks):
            here = high == c
            for f in range(SPLAT):
                source = wide(splats[f : f + 1, c * LANES : (c + 1) * LANES])
                totals[f] = jnp.where(here, lane_gather(source, low), totals[f])
        for half in range(2):
            for f in range(SPLAT):
                sent[i * 2 + half, f * 4 : f * 4 + 4, :] = totals[f][half * 4 : half * 4 + 4, :]
            sent[i * 2 + half, 36:40, :] = jnp.zeros((4, LANES), F32)

    summed = gathered[0]
    for k in range(1, gathered.shape[0]):
        summed = summed + gathered[k]
    back[...] = summed


def owner_gather(splats, wanted, gathered):
    slots = wanted.shape[1]
    return pl.pallas_call(
        owner_gather_kernel,
        out_shape=(
            jax.ShapeDtypeStruct((NEAR, 40, LANES), F32),
            jax.ShapeDtypeStruct((16, LANES), F32),
        ),
        scratch_shapes=[pltpu.VMEM((slots // LANES, LANES), jnp.int32)],
        name="owner_gather",
    )(splats, wanted, gathered)


def scatter_columns(index, values, left, right, column, bins):
    high = wide(jnp.right_shift(index, 8), 16)
    low = wide(jnp.bitwise_and(index, 255), 256)
    place = lax.broadcasted_iota(jnp.int32, (256, LANES), 0)
    right[:, pl.ds(column, LANES)] = jnp.where(place == low, 1.0, 0.0).astype(BF16)
    first = values.astype(BF16).astype(F32)
    second = values - first
    for h in range(bins):
        here = high == h
        left[h * 32 : h * 32 + 16, pl.ds(column, LANES)] = jnp.where(here, first, 0.0).astype(BF16)
        left[h * 32 + 16 : h * 32 + 32, pl.ds(column, LANES)] = jnp.where(here, second, 0.0).astype(BF16)


def scatter_product(left, right, product):
    depth = left.shape[1]
    step = 768 if depth % 768 == 0 else 1280
    product[...] = jnp.zeros_like(product)

    @pl.loop(0, depth // step)
    def _(i):
        columns = pl.ds(pl.multiple_of(i * step, LANES), step)
        product[...] += lax.dot_general(
            left[:, columns],
            right[:, columns],
            (((1,), (1,)), ((), ())),
            preferred_element_type=F32,
        )


def tiles_kernel(
    arrived,
    backs,
    tile_list,
    tile_order,
    tile_len,
    tile_pos,
    target,
    slot_grads,
    back_grads,
    order,
    live,
    entries,
    wished_in,
    wished,
    alphas,
    split,
    sums,
    terms,
    carried,
    color_sums,
    entry_grads,
    before,
    after,
    left,
    right,
    product,
):
    tiles, list_len = tile_order.shape
    groups = list_len // LANES
    lasts = groups + 1
    back_row = tiles * groups

    eight = lax.broadcasted_iota(jnp.int32, (8, LANES), 0)
    lengths = jnp.zeros((8, LANES), jnp.int32)
    for t in range(tiles):
        lengths = jnp.where(lax.rem(eight, tiles) == t, tile_len[t], lengths)
    for pair in range(groups // 2):
        ranks = jnp.concatenate(
            [
                tile_order[:, (2 * pair) * LANES : (2 * pair + 1) * LANES],
                tile_order[:, (2 * pair + 1) * LANES : (2 * pair + 2) * LANES],
            ],
            axis=0,
        )
        high = jnp.right_shift(ranks, 7)
        low = jnp.bitwise_and(ranks, LANES - 1)
        named = jnp.zeros((8, LANES), jnp.int32)
        for c in range(groups):
            part = [
                tile_list[:, t * list_len + c * LANES : t * list_len + (c + 1) * LANES]
                for t in range(tiles)
            ]
            source = jnp.concatenate(part + part, axis=0)
            named = jnp.where(high == c, lane_gather(source, low), named)
        order[pair * 8 : pair * 8 + 8, :] = named
        live[pair * 8 : pair * 8 + 8, :] = jnp.where(ranks < lengths, 1.0, 0.0)

    @pl.loop(0, back_row // 8)
    def _(i):
        spots = pl.ds(pl.multiple_of(i * 8, 8), 8)
        slots = order[spots, :]
        high = jnp.right_shift(slots, 7)
        low = jnp.bitwise_and(slots, LANES - 1)

        def window(w, totals):
            totals = list(totals)
            for k in range(4):
                here = high == w * 4 + k
                for f in range(SPLAT):
                    source = wide(arrived[w, f * 4 + k : f * 4 + k + 1, :])
                    totals[f] = jnp.where(here, lane_gather(source, low), totals[f])
            return tuple(totals)

        none = tuple(jnp.zeros((8, LANES), F32) for _ in range(SPLAT))
        totals = lax.fori_loop(0, NEAR, window, none)
        for f in range(SPLAT):
            entries[f, spots, :] = totals[f] * live[spots, :] if f == 5 else totals[f]

    summed = backs[0]
    for k in range(1, backs.shape[0]):
        summed = summed + backs[k]
    for f in range(SPLAT):
        entries[f, back_row : back_row + 1, :] = summed[f : f + 1, :]

    wished_in[...] = jnp.zeros_like(wished_in)
    for t in range(tiles):
        wished_in[3 * t : 3 * t + 3, :] = target[:, t * 256 : (t + 1) * 256]
    columns = jnp.transpose(wished_in[...])
    for t in range(tiles):
        for c in range(3):
            one = columns[:, 3 * t + c : 3 * t + c + 1]
            wished[t * 3 + c] = jnp.broadcast_to(one, (256, LANES))

    row_at = jnp.bitwise_and(lax.broadcasted_iota(jnp.int32, (256, 256), 0), LANES - 1)
    col_at = lax.broadcasted_iota(jnp.int32, (256, 256), 1)
    before[...] = jnp.where((row_at < col_at) | (col_at >= LANES), 1.0, 0.0).astype(BF16)
    after[...] = jnp.where((row_at > col_at) | (col_at >= LANES), 1.0, 0.0).astype(BF16)
    entry_grads[...] = jnp.zeros_like(entry_grads)

    def row_of(t, j):
        listed = j // 2 * 8 + lax.rem(j, 2) * 4 + t
        return jnp.where(j == groups, back_row, listed)

    def entry(f, row):
        return wide(entries[f, pl.ds(row, 1), :])

    across = (
        lax.broadcasted_iota(jnp.int32, (2, 8, LANES), 0) * 8
        + lax.broadcasted_iota(jnp.int32, (2, 8, LANES), 1)
    ).astype(F32) + 0.5

    @pl.loop(0, tiles)
    def _(t):
        place = tile_pos[t]
        corner_x = (lax.rem(place, TILES_X) * 16).astype(F32)
        corner_y = (place // TILES_X * 16).astype(F32)

        @pl.loop(0, lasts)
        def _(j):
            row = row_of(t, j)
            delta_x = (across + corner_x) - entry(0, row)[None]
            center_v = entry(1, row)
            flat = -0.5 * entry(2, row)[None] * delta_x * delta_x
            mixed = -entry(3, row)[None] * delta_x
            half_c = -0.5 * entry(4, row)
            opacity = entry(5, row)[None]
            for y in range(16):
                delta_y = (corner_y + (y + 0.5)) - center_v
                slope = half_c * delta_y
                power = (mixed + slope[None]) * delta_y[None] + flat
                alpha = opacity * jnp.exp(power)
                keep = jnp.log(1.0 - alpha)
                spot = slice(y * 16, y * 16 + 16)
                alphas[j, spot, :] = alpha.reshape(16, LANES)
                first, second = pieces_of(keep.reshape(16, LANES))
                split[j, spot, :LANES] = first
                split[j, spot, LANES:] = second

        @pl.loop(0, lasts)
        def _(j):
            sums[j] = jnp.dot(split[j], before[...], preferred_element_type=F32)

        color_sums[...] = jnp.zeros_like(color_sums)

        @pl.loop(0, 16)
        def _(y):
            spot = pl.ds(pl.multiple_of(y * 16, 16), 16)
            gone = jnp.zeros((16, LANES), F32)
            seen = [jnp.zeros((2, 8, LANES), F32) for _ in range(3)]
            weights = []
            for j in range(lasts):
                row = row_of(t, j)
                transmit = jnp.exp(gone + sums[j, spot, :LANES])
                gone = gone + sums[j, spot, LANES:]
                weight = (alphas[j, spot, :] * transmit).reshape(2, 8, LANES)
                weights.append(weight)
                for c in range(3):
                    seen[c] = seen[c] + weight * entry(6 + c, row)[None]
            slopes = []
            for c in range(3):
                color = jnp.sum(seen[c].reshape(16, LANES), axis=1, keepdims=True)
                slope = 16.0 * (color - wished[t * 3 + c, spot, :])
                slopes.append(slope.reshape(2, 8, LANES))
            for j in range(lasts):
                row = row_of(t, j)
                pull = slopes[0] * entry(6, row)[None]
                pull = pull + slopes[1] * entry(7, row)[None]
                pull = pull + slopes[2] * entry(8, row)[None]
                term = (pull * weights[j]).reshape(16, LANES)
                terms[j, spot, :] = term
                first, second = pieces_of(term)
                split[j, spot, :LANES] = first
                split[j, spot, LANES:] = second
                for c in range(3):
                    part = slopes[c] * weights[j]
                    color_sums[c, j] += part[0] + part[1]

        @pl.loop(0, lasts)
        def _(j):
            sums[j] = jnp.dot(split[j], after[...], preferred_element_type=F32)

        carried[...] = jnp.zeros_like(carried)

        @pl.loop(0, lasts)
        def _(back_j):
            j = groups - back_j
            row = row_of(t, j)
            delta_x = (across + corner_x) - entry(0, row)[None]
            center_v = entry(1, row)
            zero = jnp.zeros((2, 8, LANES), F32)
            sum_none, sum_y, sum_yy = zero, zero, zero
            for y in range(16):
                spot = slice(y * 16, y * 16 + 16)
                behind = carried[spot, :] + sums[j, spot, :LANES]
                carried[spot, :] += sums[j, spot, LANES:]
                alpha = alphas[j, spot, :]
                share = alpha / (1.0 - alpha)
                pull = (terms[j, spot, :] - behind * share).reshape(2, 8, LANES)
                delta_y = ((corner_y + (y + 0.5)) - center_v)[None]
                sum_none = sum_none + pull
                moved = pull * delta_y
                sum_y = sum_y + moved
                sum_yy = sum_yy + moved * delta_y

            def fold(value):
                return jnp.sum(value[0] + value[1], axis=0, keepdims=True)

            first_x = sum_none * delta_x
            in_none = fold(sum_none)
            in_x = fold(first_x)
            in_xx = fold(first_x * delta_x)
            in_xy = fold(sum_y * delta_x)
            in_y = fold(sum_y)
            in_yy = fold(sum_yy)
            con_a, con_b, con_c = (entries[f, pl.ds(row, 1), :] for f in (2, 3, 4))
            made = [
                con_a * in_x + con_b * in_y,
                con_c * in_y + con_b * in_x,
                -0.5 * in_xx,
                -in_xy,
                -0.5 * in_yy,
                in_none,
            ]
            made += [jnp.sum(color_sums[c, j], axis=0, keepdims=True) for c in range(3)]
            for f in range(SPLAT):
                entry_grads[row, f : f + 1, :] += made[f]

    back_grads[...] = entry_grads[back_row]

    @pl.loop(0, back_row)
    def _(r):
        column = pl.multiple_of(r * LANES, LANES)
        scatter_columns(order[pl.ds(r, 1), :], entry_grads[r], left, right, column, 2 * NEAR)

    scatter_product(left, right, product)
    for h in range(2 * NEAR):
        value = product[h * 32 : h * 32 + 16, :] + product[h * 32 + 16 : h * 32 + 32, :]
        for f in range(SPLAT):
            for half in range(2):
                at = f * 4 + (h % 2) * 2 + half
                slot_grads[h // 2, at : at + 1, :] = value[f : f + 1, half * LANES : (half + 1) * LANES]
    for w in range(NEAR):
        slot_grads[w, 36:40, :] = jnp.zeros((4, LANES), F32)


def render_tiles(arrived, backs, tile_list, tile_order, tile_len, tile_pos, target):
    tiles, list_len = tile_order.shape
    rows = tiles * list_len // LANES
    lasts = list_len // LANES + 1
    vmem = pl.BlockSpec(memory_space=pltpu.VMEM)
    smem = pl.BlockSpec(memory_space=pltpu.SMEM)
    return pl.pallas_call(
        tiles_kernel,
        out_shape=(
            jax.ShapeDtypeStruct((NEAR, 40, LANES), F32),
            jax.ShapeDtypeStruct((16, LANES), F32),
        ),
        in_specs=[vmem, vmem, vmem, vmem, smem, smem, vmem],
        out_specs=(vmem, vmem),
        scratch_shapes=[
            pltpu.VMEM((rows, LANES), jnp.int32),
            pltpu.VMEM((rows, LANES), F32),
            pltpu.VMEM((SPLAT, rows + 8, LANES), F32),
            pltpu.VMEM((LANES, 256), F32),
            pltpu.VMEM((tiles * 3, 256, LANES), F32),
            pltpu.VMEM((lasts, 256, LANES), F32),
            pltpu.VMEM((lasts, 256, 256), BF16),
            pltpu.VMEM((lasts, 256, 256), F32),
            pltpu.VMEM((lasts, 256, LANES), F32),
            pltpu.VMEM((256, LANES), F32),
            pltpu.VMEM((3, lasts, 8, LANES), F32),
            pltpu.VMEM((rows + 1, 16, LANES), F32),
            pltpu.VMEM((256, 256), BF16),
            pltpu.VMEM((256, 256), BF16),
            pltpu.VMEM((2 * NEAR * 32, rows * LANES), BF16),
            pltpu.VMEM((256, rows * LANES), BF16),
            pltpu.VMEM((2 * NEAR * 32, 256), F32),
        ],
        compiler_params=pltpu.CompilerParams(vmem_limit_bytes=48 * 2**20),
        name="render_tiles",
    )(arrived, backs, tile_list, tile_order, tile_len, tile_pos, target)


def owner_sum_kernel(returned, wanted, backs, bg_ids, grads, left, right, product):
    slots = wanted.shape[1]
    g_local = grads.shape[1]
    bins = g_local // 256
    padding = lambda count: [jnp.zeros((16 - count, LANES), F32)]

    @pl.loop(0, NEAR)
    def _(w):
        for k in range(4):
            column = pl.multiple_of((w * 4 + k) * LANES, LANES)
            rows = [returned[w, f * 4 + k : f * 4 + k + 1, :] for f in range(SPLAT)]
            values = jnp.concatenate(rows + padding(SPLAT), axis=0)
            scatter_columns(wanted[:, pl.ds(column, LANES)], values, left, right, column, bins)

    summed = backs[0]
    for k in range(1, backs.shape[0]):
        summed = summed + backs[k]
    mine = bg_ids[...] - lax.axis_index("dev") * g_local
    scatter_columns(mine, summed, left, right, slots, bins)
    left[:, slots + LANES :] = jnp.zeros((left.shape[0], LANES), BF16)
    right[:, slots + LANES :] = jnp.zeros((256, LANES), BF16)
    scatter_product(left, right, product)
    for h in range(bins):
        value = product[h * 32 : h * 32 + 16, :] + product[h * 32 + 16 : h * 32 + 32, :]
        grads[:, h * 256 : (h + 1) * 256] = value


def owner_sum(returned, wanted, backs, bg_ids, g_local):
    depth = wanted.shape[1] + 2 * LANES
    bins = g_local // 256
    return pl.pallas_call(
        owner_sum_kernel,
        out_shape=jax.ShapeDtypeStruct((16, g_local), F32),
        scratch_shapes=[
            pltpu.VMEM((bins * 32, depth), BF16),
            pltpu.VMEM((256, depth), BF16),
            pltpu.VMEM((bins * 32, 256), F32),
        ],
        compiler_params=pltpu.CompilerParams(vmem_limit_bytes=48 * 2**20),
        name="owner_sum",
    )(returned, wanted, backs, bg_ids)


def update_kernel(center_y, params, adam_m, adam_v, pulls, new_params, new_m, new_v, grads):
    chunk = params.shape[1]
    rows = [params[i : i + 1, :] for i in range(10)]
    made, pull_back = jax.vjp(lambda given: geometry(given, center_y), rows)
    color_pulls = [pulls[6 + c : 7 + c, :] for c in range(3)]
    given = [pulls[i : i + 1, :] for i in range(5)]
    for k in range(16):
        at = 11 + 3 * k
        total = color_pulls[0] * params[at : at + 1, :]
        total = total + color_pulls[1] * params[at + 1 : at + 2, :]
        total = total + color_pulls[2] * params[at + 2 : at + 3, :]
        given.append(total)
        for c in range(3):
            grads[at + c : at + c + 1, :] = made[5 + k] * color_pulls[c]
    for i, row in enumerate(pull_back(given)[0]):
        grads[i : i + 1, :] = row
    grads[10:11, :] = pulls[5:6, :] * (1.0 - jax.nn.sigmoid(params[10:11, :]))
    slope = grads[...]
    moment = 0.9 * adam_m[...] + 0.1 * slope
    spread_of = 0.999 * adam_v[...] + 0.001 * slope * slope
    update = moment / BIAS_ONE / (jnp.sqrt(spread_of / BIAS_TWO) + 1e-08)
    new_params[...] = params[...] - 0.05 * update
    new_m[...] = moment
    new_v[...] = spread_of


def update(params, adam_m, adam_v, pulls, center_y):
    count, g_local = params.shape
    chunk = 512
    block = pl.BlockSpec((count, chunk), lambda i: (0, i))
    shape = jax.ShapeDtypeStruct(params.shape, F32)
    return pl.pallas_call(
        functools.partial(update_kernel, center_y),
        grid=(g_local // chunk,),
        out_shape=(shape, shape, shape),
        in_specs=[block, block, block, pl.BlockSpec((16, chunk), lambda i: (0, i))],
        out_specs=(block, block, block),
        scratch_shapes=[pltpu.VMEM((count, chunk), F32)],
        name="update",
    )(params, adam_m, adam_v, pulls)


def per_device(
    devices,
    params,
    adam_m,
    adam_v,
    target,
    req_rows,
    tile_list,
    tile_len,
    tile_order,
    tile_pos,
    bg_ids,
):
    g_local = params.shape[1]
    tiles_here = tile_order.shape[0]
    center_y = 8.0 * (tiles_here * devices // TILES_X)
    ids = bg_ids.reshape(1, LANES)
    outer = devices // INNER
    splats, back = project_local(params, ids, center_y)
    wanted, inner_backs = communicate(
        request_kernel, 0, devices, req_rows, back, INNER, [], NEAR + INNER, pl.ANY
    )
    sent, back_part = owner_gather(splats, wanted, inner_backs)
    arrived, backs = communicate(
        supply_kernel, 1, devices, sent, back_part, outer, [], NEAR + outer, pl.ANY
    )
    slot_grads, back_grads = render_tiles(
        arrived, backs, tile_list, tile_order, tile_len, tile_pos, target
    )
    scratch = [pltpu.VMEM((INNER, 16, LANES), F32), pltpu.VMEM((16, LANES), F32)]
    returned, back_sums = communicate(
        return_kernel,
        2,
        devices,
        slot_grads,
        back_grads,
        outer,
        scratch,
        NEAR + INNER + outer,
        pltpu.VMEM,
    )
    pulls = owner_sum(returned, wanted, back_sums, ids, g_local)
    return update(params, adam_m, adam_v, pulls, center_y)


def solution(mesh):
    return jax.shard_map(
        functools.partial(per_device, mesh.shape["dev"]),
        mesh=mesh,
        in_specs=(
            P(None, "dev"),
            P(None, "dev"),
            P(None, "dev"),
            P(None, "dev"),
            P("dev", None),
            P("dev", None),
            P("dev"),
            P("dev", None),
            P("dev"),
            P(),
        ),
        out_specs=(P(None, "dev"), P(None, "dev"), P(None, "dev")),
        check_vma=False,
    )
```

profile of v0, /device:TPU:1, one launch (start us, length us, event | category | flops | bytes accessed | tf_op | source)
XLA Modules:
  0.0 115.0 jit_solution(7237608044030272027)
XLA Ops:
  0.6 5.4 %project_local.1 = (f32[16,4096]{1,0:T(8,128)}, f32[16,128]{1,0:T(8,128)}) custom-call(f32[59,4096]{1,0:T(8,128)} %params.3, s32[1,128]{1,0:T(1,128)} %bitcast.1), custom_call_target="tpu_custom_call" | custom-call | tf_op jit(solution)/shard_map/project_local/pallas_call | solution.py:162
  6.0 13.9 %request_kernel.1 = (s32[1,5120]{1,0:T(1,128)}, f32[16,16,128]{2,1,0:T(8,128)}) custom-call(s32[1,5120]{1,0:T(1,128)} %req.1, f32[16,128]{1,0:T(8,128)} %get-tuple-element.16.back), custom_call_target="tpu_custom_call" | custom-call | tf_op jit(solution)/shard_map/request_kernel/pallas_call | solution.py:294
  20.0 3.6 %owner_gather.1 = (f32[10,40,128]{2,1,0:T(8,128)}, f32[16,128]{1,0:T(8,128)}) custom-call(f32[16,4096]{1,0:T(8,128)} %get-tuple-element.15.splats, s32[1,5120]{1,0:T(1,128)} %get-tuple-element.17.wanted, f32[16,16,128]{2,1,0:T(8,128)} %get-tuple-element.18.gathered), custom_call_target="tpu_custom_call" | custom-call | tf_op jit(solution)/shard_map/owner_gather/pallas_call | solution.py:342
  23.5 0.0 copy-start.7
  23.5 0.0 copy-start.8
  23.5 0.0 copy-start.9
  23.5 11.5 %supply_kernel.1 = (f32[10,40,128]{2,1,0:T(8,128)}, f32[8,16,128]{2,1,0:T(8,128)}) custom-call(f32[10,40,128]{2,1,0:T(8,128)} %get-tuple-element.19.sent, f32[16,128]{1,0:T(8,128)} %get-tuple-element.20.back), custom_call_target="tpu_custom_call" | custom-call | tf_op jit(solution)/shard_map/supply_kernel/pallas_call | solution.py:294
  35.0 0.0 copy-start.12
  35.0 0.0 copy-start.13
  35.1 0.0 copy-done.7
  35.1 0.0 copy-done.8
  35.1 0.0 copy-done.9
  35.1 0.6 copy-done.12
  35.7 0.0 copy-done.13
  35.7 0.0 copy-start.2
  35.7 0.9 copy-done.2
  36.6 0.0 copy-start.5
  36.6 0.8 copy-done.5
  37.5 46.3 %render_tiles.1 = (f32[10,40,128]{2,1,0:T(8,128)S(1)}, f32[16,128]{1,0:T(8,128)S(1)}) custom-call(f32[10,40,128]{2,1,0:T(8,128)S(1)} %copy-done.2, f32[8,16,128]{2,1,0:T(8,128)S(1)} %copy-done.5, s32[1,5120]{1,0:T(1,128)S(1)} %copy-done.7, s32[4,1280]{1,0:T(4,128)S(1)} %copy-done.8, s32[4]{0:T(128)S(1)} %copy-done.12, s32[4]{0:T(128)S(1)} %copy-done.13, ...), custom_call_target="tpu_custom_call" | custom-call | tf_op jit(solution)/shard_map/render_tiles/pallas_call | solution.py:634
  83.8 0.0 copy-start.3
  83.8 0.7 copy-done.3
  84.5 0.0 copy-start.10
  84.5 0.6 copy-done.10
  85.1 0.0 copy-start.4
  85.1 15.1 %return_kernel.1 = (f32[10,40,128]{2,1,0:T(8,128)}, f32[8,16,128]{2,1,0:T(8,128)}) custom-call(f32[10,40,128]{2,1,0:T(8,128)} %copy-done.3, f32[16,128]{1,0:T(8,128)} %copy-done.10), custom_call_target="tpu_custom_call" | custom-call | tf_op jit(solution)/shard_map/return_kernel/pallas_call | solution.py:294
  100.2 0.0 copy-start.11
  100.2 0.0 copy-done.4
  100.2 0.6 copy-done.11
  100.9 0.0 copy-start.1
  100.9 0.9 copy-done.1
  101.8 0.0 copy-start.6
  101.8 0.8 copy-done.6
  102.6 4.9 %owner_sum.1.pulls = f32[16,4096]{1,0:T(8,128)S(1)} custom-call(f32[10,40,128]{2,1,0:T(8,128)S(1)} %copy-done.1, s32[1,5120]{1,0:T(1,128)S(1)} %copy-done.4, f32[8,16,128]{2,1,0:T(8,128)S(1)} %copy-done.6, s32[1,128]{1,0:T(1,128)S(1)} %bitcast.2), custom_call_target="tpu_custom_call" | custom-call | tf_op jit(solution)/shard_map/owner_sum/pallas_call | solution.py:696
  107.6 0.0 copy-start
  107.6 0.7 copy-done
  108.3 6.7 %update.1 = (f32[59,4096]{1,0:T(8,128)}, f32[59,4096]{1,0:T(8,128)}, f32[59,4096]{1,0:T(8,128)}) custom-call(f32[59,4096]{1,0:T(8,128)} %params.3, f32[59,4096]{1,0:T(8,128)} %adam_m.1, f32[59,4096]{1,0:T(8,128)} %adam_v.1, f32[16,4096]{1,0:T(8,128)} %copy-done), custom_call_target="tpu_custom_call" | custom-call | tf_op jit(solution)/shard_map/update/pallas_call | solution.py:740
Async XLA Ops:
  23.5 11.5 %copy-start.7 = (s32[1,5120]{1,0:T(1,128)S(1)}, s32[1,5120]{1,0:T(1,128)}, u32[]{:S(2)}) copy-start(s32[1,5120]{1,0:T(1,128)} %tile_list.1) | copy-start | bytes 61444
  23.5 11.5 %copy-start.8 = (s32[4,1280]{1,0:T(4,128)S(1)}, s32[4,1280]{1,0:T(4,128)}, u32[]{:S(2)}) copy-start(s32[4,1280]{1,0:T(4,128)} %tile_order.1) | copy-start | bytes 61444
  23.5 11.5 %copy-start.9 = (f32[3,1024]{1,0:T(4,128)S(1)}, f32[3,1024]{1,0:T(4,128)}, u32[]{:S(2)}) copy-start(f32[3,1024]{1,0:T(4,128)} %target.1) | copy-start | bytes 36868
  35.0 0.7 copy-start.12
  35.0 0.7 copy-start.13
  35.7 0.9 copy-start.2
  36.6 0.8 copy-start.5
  83.8 0.7 copy-start.3
  84.5 0.6 copy-start.10
  85.1 15.1 %copy-start.4 = (s32[1,5120]{1,0:T(1,128)S(1)}, s32[1,5120]{1,0:T(1,128)}, u32[]{:S(2)}) copy-start(s32[1,5120]{1,0:T(1,128)} %get-tuple-element.17.wanted) | copy-start | bytes 61444
  100.2 0.7 copy-start.11
  100.9 0.9 copy-start.1
  101.8 0.8 copy-start.6
  107.6 0.7 copy-start
where the time goes:
time: 116 us; the launch traced here: 115 us
  Pallas kernels  107 us (92%)
  local copies, waits for them, and re-layouts  6.77 us (6%)
    pallas_call x1, Pallas kernels, render_tiles(): pl.pallas_call(tiles_kernel, out_shape=(jax.ShapeDtypeStruct((NEAR, 40, L...  46.3 us
    pallas_call x3, Pallas kernels, communicate(): pl.pallas_call(functools.partial(kernel, devices), out_shape=(jax.ShapeDt...  40.5 us
    unnamed x28, local copies, waits for them, and re-layouts  6.77 us
    pallas_call x1, Pallas kernels, update(): pl.pallas_call(functools.partial(update_kernel, center_y), grid=(g_local...  6.73 us
    pallas_call x1, Pallas kernels, project_local(): pl.pallas_call(functools.partial(project_kernel, center_y), grid=(g_local...  5.38 us
    pallas_call x1, Pallas kernels, owner_sum(): pl.pallas_call(owner_sum_kernel, out_shape=jax.ShapeDtypeStruct((16, g_lo...  4.95 us
    pallas_call x1, Pallas kernels, owner_gather(): pl.pallas_call(owner_gather_kernel, out_shape=(jax.ShapeDtypeStruct((NEAR...  3.57 us

commit v1 on v0

v1 whole, which is shorter than its diff:
```python
import functools

import jax
import jax.numpy as jnp
from jax import lax
from jax.experimental import pallas as pl
from jax.experimental.pallas import tpu as pltpu
from jax.sharding import PartitionSpec as P

TILES_X = 32
NEAR = 10
FOCAL = 512.0
BIAS_ONE = 1.0 - 0.9**10
BIAS_TWO = 1.0 - 0.999**10
MESH = pl.DeviceIdType.MESH
F32 = jnp.float32
BF16 = jnp.bfloat16
LANES = 128
INNER = 16
SPLAT = 9


def harmonics(dir_x, dir_y, dir_z):
    sq_x = dir_x * dir_x
    sq_y = dir_y * dir_y
    sq_z = dir_z * dir_z
    return [
        0.28209479177387814 + 0.0 * dir_x,
        -0.4886025119029199 * dir_y,
        0.4886025119029199 * dir_z,
        -0.4886025119029199 * dir_x,
        1.0925484305920792 * dir_x * dir_y,
        -1.0925484305920792 * dir_y * dir_z,
        0.31539156525252005 * (2.0 * sq_z - sq_x - sq_y),
        -1.0925484305920792 * dir_x * dir_z,
        0.5462742152960396 * (sq_x - sq_y),
        -0.5900435899266435 * dir_y * (3.0 * sq_x - sq_y),
        2.890611442640554 * dir_x * dir_y * dir_z,
        -0.4570457994644658 * dir_y * (4.0 * sq_z - sq_x - sq_y),
        0.3731763325901154 * dir_z * (2.0 * sq_z - 3.0 * sq_x - 3.0 * sq_y),
        -0.4570457994644658 * dir_x * (4.0 * sq_z - sq_x - sq_y),
        1.445305721320277 * dir_z * (sq_x - sq_y),
        -0.5900435899266435 * dir_x * (sq_x - 3.0 * sq_y),
    ]


def geometry(rows, center_y):
    pos_x, pos_y, depth = (rows[0], rows[1], rows[2])
    stretches = (jnp.exp(rows[3]), jnp.exp(rows[4]), jnp.exp(rows[5]))
    quat_norm = jnp.sqrt(
        rows[6] * rows[6] + rows[7] * rows[7] + rows[8] * rows[8] + rows[9] * rows[9]
    )
    inv_norm = 1.0 / quat_norm
    quat_w = rows[6] * inv_norm
    quat_x = rows[7] * inv_norm
    quat_y = rows[8] * inv_norm
    quat_z = rows[9] * inv_norm
    rotation = (
        (
            1.0 - 2.0 * (quat_y * quat_y + quat_z * quat_z),
            2.0 * (quat_x * quat_y - quat_w * quat_z),
            2.0 * (quat_x * quat_z + quat_w * quat_y),
        ),
        (
            2.0 * (quat_x * quat_y + quat_w * quat_z),
            1.0 - 2.0 * (quat_x * quat_x + quat_z * quat_z),
            2.0 * (quat_y * quat_z - quat_w * quat_x),
        ),
        (
            2.0 * (quat_x * quat_z - quat_w * quat_y),
            2.0 * (quat_y * quat_z + quat_w * quat_x),
            1.0 - 2.0 * (quat_x * quat_x + quat_y * quat_y),
        ),
    )
    inv_depth = 1.0 / depth
    focal_z = FOCAL * inv_depth
    slope_x = pos_x * inv_depth
    slope_y = pos_y * inv_depth
    cov_a = 0.3
    cov_b = 0.0
    cov_c = 0.3
    for column in range(3):
        axis_x = rotation[0][column] * stretches[column]
        axis_y = rotation[1][column] * stretches[column]
        axis_z = rotation[2][column] * stretches[column]
        image_u = focal_z * (axis_x - slope_x * axis_z)
        image_v = focal_z * (axis_y - slope_y * axis_z)
        cov_a = cov_a + image_u * image_u
        cov_b = cov_b + image_u * image_v
        cov_c = cov_c + image_v * image_v
    inv_determ = 1.0 / (cov_a * cov_c - cov_b * cov_b)
    center_u = FOCAL * slope_x + 8.0 * TILES_X
    center_v = FOCAL * slope_y + center_y
    inv_distance = 1.0 / jnp.sqrt(pos_x * pos_x + pos_y * pos_y + depth * depth)
    basis = harmonics(pos_x * inv_distance, pos_y * inv_distance, depth * inv_distance)
    conic = [cov_c * inv_determ, -cov_b * inv_determ, cov_a * inv_determ]
    return [center_u, center_v] + conic + basis


def lane_gather(source, index):
    numbers = lax.GatherDimensionNumbers(
        offset_dims=(),
        collapsed_slice_dims=(1,),
        start_index_map=(1,),
        operand_batching_dims=(0,),
        start_indices_batching_dims=(0,),
    )
    return lax.gather(
        source,
        index[..., None],
        numbers,
        (1, 1),
        mode=lax.GatherScatterMode.PROMISE_IN_BOUNDS,
    )


def wide(row, rows=8):
    return jnp.broadcast_to(row, (rows, row.shape[-1]))


def pieces_of(value):
    first = value.astype(BF16)
    return first, (value - first.astype(F32)).astype(BF16)


def offsets_of(devices):
    lines = [0, 1, -1, 4, -4]
    return [(lines[w % 5] + w // 5 * (devices // 2)) % devices for w in range(NEAR)]


def window_copy(devices, w, direction, given, taken, send_sem, recv_sem, local_sem):
    offset = offsets_of(devices)[w]
    if offset == 0:
        return pltpu.make_async_copy(given, taken, local_sem)
    ahead = (offset * direction) % devices
    return pltpu.make_async_remote_copy(
        src_ref=given,
        dst_ref=taken,
        send_sem=send_sem.at[w],
        recv_sem=recv_sem.at[w],
        device_id=(lax.rem(lax.axis_index("dev") + ahead, devices),),
        device_id_type=MESH,
    )


def inner_partner(devices, me, k):
    return me // INNER * INNER + lax.rem(lax.rem(me, INNER) + k, INNER)


def outer_partner(devices, me, k):
    return lax.rem(me + INNER * k, devices)


def spread(devices, count, partner, given, taken, send_sem, recv_sem):
    return [
        pltpu.make_async_remote_copy(
            src_ref=given,
            dst_ref=taken.at[k],
            send_sem=send_sem.at[k],
            recv_sem=recv_sem.at[k],
            device_id=(partner(devices, lax.axis_index("dev"), k),),
            device_id_type=MESH,
        )
        for k in range(1, count)
    ]


def greet(devices):
    me = lax.axis_index("dev")
    partners = [lax.rem(me + offset, devices) for offset in offsets_of(devices) if offset]
    partners += [inner_partner(devices, me, k) for k in range(1, INNER)]
    partners += [outer_partner(devices, me, k) for k in range(1, devices // INNER)]
    barrier = pltpu.get_barrier_semaphore()
    for partner in partners:
        pl.semaphore_signal(barrier, inc=1, device_id=(partner,), device_id_type=MESH)
    return lambda: pl.semaphore_wait(barrier, len(partners))


def start(copies):
    for copy in copies:
        copy.start()


def finish(copies):
    for copy in copies:
        copy.wait()


def exchange_semaphores(devices):
    return [
        pltpu.SemaphoreType.DMA((NEAR,)),
        pltpu.SemaphoreType.DMA((NEAR,)),
        pltpu.SemaphoreType.DMA((INNER,)),
        pltpu.SemaphoreType.DMA((INNER,)),
        pltpu.SemaphoreType.DMA((devices // INNER,)),
        pltpu.SemaphoreType.DMA((devices // INNER,)),
        pltpu.SemaphoreType.DMA((3,)),
    ]


def feature(laid, f, block):
    first = (block // 2 * 16 + block % 2) * 8 + f % 8
    return laid[f // 8, pl.ds(first, 8, stride=16), :]


def lay_out(params, laid):
    count, g_local = params.shape

    @pl.loop(0, g_local // LANES)
    def _(c):
        columns = pl.ds(pl.multiple_of(c * LANES, LANES), LANES)
        first = pl.multiple_of(c * 8, 8)
        for group in range(count // 8):
            laid[group, pl.ds(first, 8), :] = params[group * 8 : group * 8 + 8, columns]
        over = count % 8
        laid[count // 8, pl.ds(first, over), :] = params[count - over :, columns]


def front_kernel(
    devices,
    center_y,
    params,
    bg_ids,
    req,
    arrived,
    backs,
    wanted,
    laid,
    splats,
    back,
    held,
    part,
    sent,
    index,
    ask_send,
    ask_recv,
    send_sem,
    recv_sem,
    inner_send,
    inner_recv,
    outer_send,
    outer_recv,
    local_sem,
):
    count, g_local = params.shape
    chunks = g_local // LANES
    cap = req.shape[1] // NEAR
    greeted = greet(devices)
    lay_out(params, laid)

    def project(block):
        rows = [feature(laid, f, block) for f in range(11)]
        made = geometry(rows, center_y)
        opacity = jax.nn.sigmoid(rows[10])
        colors = []
        for c in range(3):
            total = made[5] * feature(laid, 11 + c, block)
            for k in range(1, 16):
                total = total + made[5 + k] * feature(laid, 11 + 3 * k + c, block)
            colors.append(total + 0.5)
        for f, row in enumerate(made[:5] + [opacity] + colors):
            splats[f, block % 2, block // 2 * 8 : block // 2 * 8 + 8, :] = row

    project(0)
    greeted()
    asks = []
    for w in range(NEAR):
        columns = pl.ds(w * cap, cap)
        asks.append(
            window_copy(
                devices, w, 1, req.at[:, columns], wanted.at[:, columns], ask_send, ask_recv, local_sem.at[0]
            )
        )
    start(asks)
    for block in range(1, chunks // 8):
        project(block)

    local = wide(bg_ids[...] - lax.axis_index("dev") * g_local)
    high = jnp.right_shift(local, 7)
    low = jnp.bitwise_and(local, LANES - 1)
    eight = lax.broadcasted_iota(jnp.int32, (8, LANES), 0)
    back[...] = jnp.zeros_like(back)
    for f in range(SPLAT):
        total = jnp.zeros((8, LANES), F32)
        for block in range(chunks // 8):
            hb, half = block // 2, block % 2
            found = lane_gather(splats[f, half, hb * 8 : hb * 8 + 8, :], low)
            total = jnp.where(high == hb * 16 + 2 * eight + half, found, total)
        back[f : f + 1, :] = jnp.sum(total, axis=0, keepdims=True)
    inner = spread(devices, INNER, inner_partner, back, held, inner_send, inner_recv)
    start(inner)

    finish(asks)
    for r in range(wanted.shape[1] // LANES):
        index[r : r + 1, :] = wanted[:, r * LANES : (r + 1) * LANES]
    sends = []
    outer = []
    for i in reversed(range(NEAR // 2)):
        rows = index[i * 8 : i * 8 + 8, :]
        high = jnp.right_shift(rows, 7)
        low = jnp.bitwise_and(rows, LANES - 1)

        def pick(step, totals, high=high, low=low):
            totals = list(totals)
            for k in range(4):
                for half in range(2):
                    c = step * 4 + k
                    here = high == 2 * c + half
                    for f in range(SPLAT):
                        source = wide(splats[f, half, pl.ds(c, 1), :])
                        totals[f] = jnp.where(here, lane_gather(source, low), totals[f])
            return tuple(totals)

        none = tuple(jnp.zeros((8, LANES), F32) for _ in range(SPLAT))
        totals = lax.fori_loop(0, chunks // 8, pick, none)
        for half in range(2):
            w = i * 2 + half
            for f in range(SPLAT):
                sent[w, f * 4 : f * 4 + 4, :] = totals[f][half * 4 : half * 4 + 4, :]
            sent[w, 36:40, :] = jnp.zeros((4, LANES), F32)
            sends.append(
                window_copy(
                    devices, w, -1, sent.at[w], arrived.at[w], send_sem, recv_sem, local_sem.at[1]
                )
            )
        start(sends[-2:])
        if i == NEAR // 2 - 2:
            finish(inner)
            summed = back[...]
            for k in range(1, INNER):
                summed = summed + held[k]
            part[...] = summed
            outer = spread(
                devices, devices // INNER, outer_partner, part, backs, outer_send, outer_recv
            )
            start(outer)
            backs[0] = summed
    finish(outer)
    finish(sends)


def supply(devices, params, bg_ids, req_rows, center_y):
    count, g_local = params.shape
    slots = req_rows.shape[1]
    vmem = pl.BlockSpec(memory_space=pltpu.VMEM)
    return pl.pallas_call(
        functools.partial(front_kernel, devices, center_y),
        out_shape=(
            jax.ShapeDtypeStruct((NEAR, 40, LANES), F32),
            jax.ShapeDtypeStruct((devices // INNER, 16, LANES), F32),
            jax.ShapeDtypeStruct((1, slots), jnp.int32),
        ),
        in_specs=[vmem] * 3,
        out_specs=(vmem,) * 3,
        scratch_shapes=[
            pltpu.VMEM((8, g_local // 16, LANES), F32),
            pltpu.VMEM((SPLAT, 2, g_local // 256, LANES), F32),
            pltpu.VMEM((16, LANES), F32),
            pltpu.VMEM((INNER, 16, LANES), F32),
            pltpu.VMEM((16, LANES), F32),
            pltpu.VMEM((NEAR, 40, LANES), F32),
            pltpu.VMEM((slots // LANES, LANES), jnp.int32),
            pltpu.SemaphoreType.DMA((NEAR,)),
            pltpu.SemaphoreType.DMA((NEAR,)),
        ]
        + exchange_semaphores(devices),
        compiler_params=pltpu.CompilerParams(
            collective_id=0, has_side_effects=True, vmem_limit_bytes=48 * 2**20
        ),
        name="supply",
    )(params, bg_ids, req_rows)


def scatter_rows(bins):
    return 16 * (bins + -(-bins // 8))


def scatter_columns(index, eight, ninth, left, right, column, bins):
    high = wide(jnp.right_shift(index, 8))
    low = wide(jnp.bitwise_and(index, 255), 256)
    place = lax.broadcasted_iota(jnp.int32, (256, LANES), 0)
    right[:, pl.ds(column, LANES)] = jnp.where(place == low, 1.0, 0.0).astype(BF16)

    def put(at, here, value):
        first = value.astype(BF16).astype(F32)
        both = [jnp.where(here, first, 0.0), jnp.where(here, value - first, 0.0)]
        left[at : at + 16, pl.ds(column, LANES)] = jnp.concatenate(both, axis=0).astype(BF16)

    for h in range(bins):
        put(h * 16, high == h, eight)
    ninth = wide(ninth)
    for i in range(-(-bins // 8)):
        own = lax.broadcasted_iota(jnp.int32, (8, LANES), 0) + 8 * i
        put((bins + i) * 16, high == own, ninth)


def bin_values(product, half, h, bins):
    eight = product[half, h * 16 : h * 16 + 8, :] + product[half, h * 16 + 8 : h * 16 + 16, :]
    at = (bins + h // 8) * 16 + h % 8
    return eight, product[half, at : at + 1, :] + product[half, at + 8 : at + 9, :]


def scatter_product(left, right, product):
    depth = left.shape[1]
    step = 768 if depth % 768 == 0 else 1280
    product[...] = jnp.zeros_like(product)

    @pl.loop(0, depth // step)
    def _(i):
        columns = pl.ds(pl.multiple_of(i * step, LANES), step)
        made = lax.dot_general(
            left[:, columns],
            right[:, columns],
            (((1,), (1,)), ((), ())),
            preferred_element_type=F32,
        )
        product[0] += made[:, :LANES]
        product[1] += made[:, LANES:]


def tiles_kernel(
    arrived,
    backs,
    tile_list,
    tile_order,
    tile_len,
    tile_pos,
    target,
    slot_grads,
    back_grads,
    order,
    live,
    entries,
    wished_in,
    wished,
    alphas,
    split,
    sums,
    terms,
    carried,
    slopes,
    color_sums,
    entry_grads,
    before,
    after,
    left,
    right,
    product,
):
    tiles, list_len = tile_order.shape
    groups = list_len // LANES
    lasts = groups + 1
    back_row = tiles * groups

    eight = lax.broadcasted_iota(jnp.int32, (8, LANES), 0)
    lengths = jnp.zeros((8, LANES), jnp.int32)
    for t in range(tiles):
        lengths = jnp.where(lax.rem(eight, tiles) == t, tile_len[t], lengths)
    for pair in range(groups // 2):
        ranks = jnp.concatenate(
            [
                tile_order[:, (2 * pair) * LANES : (2 * pair + 1) * LANES],
                tile_order[:, (2 * pair + 1) * LANES : (2 * pair + 2) * LANES],
            ],
            axis=0,
        )
        high = jnp.right_shift(ranks, 7)
        low = jnp.bitwise_and(ranks, LANES - 1)
        named = jnp.zeros((8, LANES), jnp.int32)
        for c in range(groups):
            part = [
                tile_list[:, t * list_len + c * LANES : t * list_len + (c + 1) * LANES]
                for t in range(tiles)
            ]
            source = jnp.concatenate(part + part, axis=0)
            named = jnp.where(high == c, lane_gather(source, low), named)
        order[pair * 8 : pair * 8 + 8, :] = named
        live[pair * 8 : pair * 8 + 8, :] = jnp.where(ranks < lengths, 1.0, 0.0)

    @pl.loop(0, back_row // 8)
    def _(i):
        spots = pl.ds(pl.multiple_of(i * 8, 8), 8)
        slots = order[spots, :]
        high = jnp.right_shift(slots, 7)
        low = jnp.bitwise_and(slots, LANES - 1)

        def window(w, totals):
            totals = list(totals)
            for k in range(4):
                here = high == w * 4 + k
                for f in range(SPLAT):
                    source = wide(arrived[w, f * 4 + k : f * 4 + k + 1, :])
                    totals[f] = jnp.where(here, lane_gather(source, low), totals[f])
            return tuple(totals)

        none = tuple(jnp.zeros((8, LANES), F32) for _ in range(SPLAT))
        totals = lax.fori_loop(0, NEAR, window, none)
        for f in range(SPLAT):
            entries[f, spots, :] = totals[f] * live[spots, :] if f == 5 else totals[f]

    summed = backs[0]
    for k in range(1, backs.shape[0]):
        summed = summed + backs[k]
    for f in range(SPLAT):
        entries[f, back_row : back_row + 1, :] = summed[f : f + 1, :]

    wished_in[...] = jnp.zeros_like(wished_in)
    for t in range(tiles):
        wished_in[3 * t : 3 * t + 3, :] = target[:, t * 256 : (t + 1) * 256]
    columns = jnp.transpose(wished_in[...])
    for t in range(tiles):
        for c in range(3):
            one = columns[:, 3 * t + c : 3 * t + c + 1]
            wished[t * 3 + c] = jnp.broadcast_to(one, (256, LANES))

    row_at = jnp.bitwise_and(lax.broadcasted_iota(jnp.int32, (256, 256), 0), LANES - 1)
    col_at = lax.broadcasted_iota(jnp.int32, (256, 256), 1)
    before[...] = jnp.where((row_at < col_at) | (col_at >= LANES), 1.0, 0.0).astype(BF16)
    after[...] = jnp.where((row_at > col_at) | (col_at >= LANES), 1.0, 0.0).astype(BF16)
    entry_grads[...] = jnp.zeros_like(entry_grads)

    def row_of(t, j):
        listed = j // 2 * 8 + lax.rem(j, 2) * 4 + t
        return jnp.where(j == groups, back_row, listed)

    def entry(f, row):
        return wide(entries[f, pl.ds(row, 1), :])

    across = (
        lax.broadcasted_iota(jnp.int32, (2, 8, LANES), 0) * 8
        + lax.broadcasted_iota(jnp.int32, (2, 8, LANES), 1)
    ).astype(F32) + 0.5

    @pl.loop(0, tiles)
    def _(t):
        place = tile_pos[t]
        corner_x = (lax.rem(place, TILES_X) * 16).astype(F32)
        corner_y = (place // TILES_X * 16).astype(F32)

        @pl.loop(0, lasts)
        def _(j):
            row = row_of(t, j)
            delta_x = (across + corner_x) - entry(0, row)[None]
            center_v = entry(1, row)
            flat = -0.5 * entry(2, row)[None] * delta_x * delta_x
            mixed = -entry(3, row)[None] * delta_x
            half_c = -0.5 * entry(4, row)
            opacity = entry(5, row)[None]
            for y in range(16):
                delta_y = (corner_y + (y + 0.5)) - center_v
                slope = half_c * delta_y
                power = (mixed + slope[None]) * delta_y[None] + flat
                alpha = opacity * jnp.exp(power)
                keep = jnp.log(1.0 - alpha)
                spot = slice(y * 16, y * 16 + 16)
                alphas[j, spot, :] = alpha.reshape(16, LANES)
                first, second = pieces_of(keep.reshape(16, LANES))
                split[j, spot, :LANES] = first
                split[j, spot, LANES:] = second

        for j in range(lasts):
            sums[j] = jnp.dot(split[j], before[...], preferred_element_type=F32)

        @pl.loop(0, 8)
        def _(y):
            spot = pl.ds(pl.multiple_of(y * 32, 32), 32)
            gone = jnp.zeros((32, LANES), F32)
            seen = [jnp.zeros((4, 8, LANES), F32) for _ in range(3)]
            for j in range(lasts):
                row = row_of(t, j)
                transmit = jnp.exp(gone + sums[j, spot, :LANES])
                gone = gone + sums[j, spot, LANES:]
                weight = alphas[j, spot, :] * transmit
                terms[j, spot, :] = weight
                for c in range(3):
                    seen[c] = seen[c] + weight.reshape(4, 8, LANES) * entry(6 + c, row)[None]
            for c in range(3):
                slopes[c, spot, :] = seen[c].reshape(32, LANES)

        for c in range(3):
            color = jnp.sum(slopes[c], axis=1, keepdims=True)
            slopes[c] = 16.0 * (color - wished[t * 3 + c])

        @pl.loop(0, lasts)
        def _(j):
            row = row_of(t, j)
            colors = [entry(6 + c, row)[None] for c in range(3)]
            painted = [jnp.zeros((2, 8, LANES), F32) for _ in range(3)]
            for y in range(16):
                spot = slice(y * 16, y * 16 + 16)
                weight = terms[j, spot, :].reshape(2, 8, LANES)
                slope = [slopes[c, spot, :].reshape(2, 8, LANES) for c in range(3)]
                pull = slope[0] * colors[0] + slope[1] * colors[1] + slope[2] * colors[2]
                term = (pull * weight).reshape(16, LANES)
                terms[j, spot, :] = term
                first, second = pieces_of(term)
                split[j, spot, :LANES] = first
                split[j, spot, LANES:] = second
                for c in range(3):
                    painted[c] = painted[c] + slope[c] * weight
            for c in range(3):
                color_sums[c, j] = painted[c][0] + painted[c][1]

        for j in range(lasts):
            sums[j] = jnp.dot(split[j], after[...], preferred_element_type=F32)

        carried[...] = jnp.zeros_like(carried)

        @pl.loop(0, lasts)
        def _(back_j):
            j = groups - back_j
            row = row_of(t, j)
            delta_x = (across + corner_x) - entry(0, row)[None]
            center_v = entry(1, row)
            zero = jnp.zeros((2, 8, LANES), F32)
            sum_none, sum_y, sum_yy = zero, zero, zero
            for y in range(16):
                spot = slice(y * 16, y * 16 + 16)
                behind = carried[spot, :] + sums[j, spot, :LANES]
                carried[spot, :] += sums[j, spot, LANES:]
                alpha = alphas[j, spot, :]
                share = alpha / (1.0 - alpha)
                pull = (terms[j, spot, :] - behind * share).reshape(2, 8, LANES)
                delta_y = ((corner_y + (y + 0.5)) - center_v)[None]
                sum_none = sum_none + pull
                moved = pull * delta_y
                sum_y = sum_y + moved
                sum_yy = sum_yy + moved * delta_y

            def fold(value):
                return jnp.sum(value[0] + value[1], axis=0, keepdims=True)

            first_x = sum_none * delta_x
            in_none = fold(sum_none)
            in_x = fold(first_x)
            in_xx = fold(first_x * delta_x)
            in_xy = fold(sum_y * delta_x)
            in_y = fold(sum_y)
            in_yy = fold(sum_yy)
            con_a, con_b, con_c = (entries[f, pl.ds(row, 1), :] for f in (2, 3, 4))
            made = [
                con_a * in_x + con_b * in_y,
                con_c * in_y + con_b * in_x,
                -0.5 * in_xx,
                -in_xy,
                -0.5 * in_yy,
                in_none,
            ]
            made += [jnp.sum(color_sums[c, j], axis=0, keepdims=True) for c in range(3)]
            for f in range(SPLAT):
                entry_grads[row, f : f + 1, :] += made[f]

    back_grads[...] = entry_grads[back_row]

    @pl.loop(0, back_row)
    def _(r):
        column = pl.multiple_of(r * LANES, LANES)
        values = entry_grads[r]
        scatter_columns(
            order[pl.ds(r, 1), :], values[0:8], values[8:9], left, right, column, 2 * NEAR
        )

    scatter_product(left, right, product)
    for h in range(2 * NEAR):
        for half in range(2):
            eight, ninth = bin_values(product, half, h, 2 * NEAR)
            for f in range(SPLAT):
                at = f * 4 + (h % 2) * 2 + half
                slot_grads[h // 2, at : at + 1, :] = eight[f : f + 1] if f < 8 else ninth
    for w in range(NEAR):
        slot_grads[w, 36:40, :] = jnp.zeros((4, LANES), F32)


def render_tiles(arrived, backs, tile_list, tile_order, tile_len, tile_pos, target):
    tiles, list_len = tile_order.shape
    rows = tiles * list_len // LANES
    lasts = list_len // LANES + 1
    vmem = pl.BlockSpec(memory_space=pltpu.VMEM)
    smem = pl.BlockSpec(memory_space=pltpu.SMEM)
    return pl.pallas_call(
        tiles_kernel,
        out_shape=(
            jax.ShapeDtypeStruct((NEAR, 40, LANES), F32),
            jax.ShapeDtypeStruct((16, LANES), F32),
        ),
        in_specs=[vmem, vmem, vmem, vmem, smem, smem, vmem],
        out_specs=(vmem, vmem),
        scratch_shapes=[
            pltpu.VMEM((rows, LANES), jnp.int32),
            pltpu.VMEM((rows, LANES), F32),
            pltpu.VMEM((SPLAT, rows + 8, LANES), F32),
            pltpu.VMEM((LANES, 256), F32),
            pltpu.VMEM((tiles * 3, 256, LANES), F32),
            pltpu.VMEM((lasts, 256, LANES), F32),
            pltpu.VMEM((lasts, 256, 256), BF16),
            pltpu.VMEM((lasts, 256, 256), F32),
            pltpu.VMEM((lasts, 256, LANES), F32),
            pltpu.VMEM((256, LANES), F32),
            pltpu.VMEM((3, 256, LANES), F32),
            pltpu.VMEM((3, lasts, 8, LANES), F32),
            pltpu.VMEM((rows + 1, 16, LANES), F32),
            pltpu.VMEM((256, 256), BF16),
            pltpu.VMEM((256, 256), BF16),
            pltpu.VMEM((scatter_rows(2 * NEAR), rows * LANES), BF16),
            pltpu.VMEM((256, rows * LANES), BF16),
            pltpu.VMEM((2, scatter_rows(2 * NEAR), LANES), F32),
        ],
        compiler_params=pltpu.CompilerParams(vmem_limit_bytes=48 * 2**20),
        name="render_tiles",
    )(arrived, backs, tile_list, tile_order, tile_len, tile_pos, target)


def back_kernel(
    devices,
    g_local,
    grads,
    back,
    wanted,
    bg_ids,
    pulls,
    returned,
    gathered,
    held,
    part,
    left,
    right,
    product,
    send_sem,
    recv_sem,
    inner_send,
    inner_recv,
    outer_send,
    outer_recv,
    local_sem,
):
    bins = g_local // 256
    slots = wanted.shape[1]
    greet(devices)()
    inner = spread(devices, INNER, inner_partner, back, held, inner_send, inner_recv)
    start(inner)
    order = [9, 8, 7, 6, 5, 4, 3, 2, 1]
    copies = {
        w: window_copy(
            devices, w, 1, grads.at[w], returned.at[w], send_sem, recv_sem, local_sem.at[0]
        )
        for w in order
    }
    start(copies.values())

    def columns_of(w, source):
        for k in range(4):
            column = (w * 4 + k) * LANES
            eight = source[w, pl.ds(k, 8, stride=4), :]
            ninth = source[w, 32 + k : 33 + k, :]
            scatter_columns(
                wanted[:, column : column + LANES], eight, ninth, left, right, column, bins
            )

    columns_of(0, grads)
    finish(inner)
    summed = back[...]
    for k in range(1, INNER):
        summed = summed + held[k]
    part[...] = summed
    outer = spread(devices, devices // INNER, outer_partner, part, gathered, outer_send, outer_recv)
    start(outer)
    for w in reversed(order):
        copies[w].wait()
        columns_of(w, returned)
    finish(outer)
    summed = part[...]
    for k in range(1, devices // INNER):
        summed = summed + gathered[k]
    mine = bg_ids[...] - lax.axis_index("dev") * g_local
    scatter_columns(mine, summed[0:8], summed[8:9], left, right, slots, bins)
    left[:, slots + LANES :] = jnp.zeros((left.shape[0], LANES), BF16)
    right[:, slots + LANES :] = jnp.zeros((256, LANES), BF16)
    scatter_product(left, right, product)
    for hb in range(bins // 8):
        for half in range(2):
            spot = slice(hb * 8, hb * 8 + 8)
            for f in range(8):
                first = product[half, pl.ds(hb * 128 + f, 8, stride=16), :]
                second = product[half, pl.ds(hb * 128 + 8 + f, 8, stride=16), :]
                pulls[f, half, spot, :] = first + second
            at = (bins + hb) * 16
            ninth = product[half, at : at + 8, :] + product[half, at + 8 : at + 16, :]
            pulls[8, half, spot, :] = ninth


def collect(devices, slot_grads, back_grads, wanted, bg_ids, g_local):
    depth = wanted.shape[1] + 2 * LANES
    bins = g_local // 256
    vmem = pl.BlockSpec(memory_space=pltpu.VMEM)
    return pl.pallas_call(
        functools.partial(back_kernel, devices, g_local),
        out_shape=jax.ShapeDtypeStruct((SPLAT, 2, bins, LANES), F32),
        in_specs=[vmem] * 4,
        out_specs=vmem,
        scratch_shapes=[
            pltpu.VMEM((NEAR, 40, LANES), F32),
            pltpu.VMEM((devices // INNER, 16, LANES), F32),
            pltpu.VMEM((INNER, 16, LANES), F32),
            pltpu.VMEM((16, LANES), F32),
            pltpu.VMEM((scatter_rows(bins), depth), BF16),
            pltpu.VMEM((256, depth), BF16),
            pltpu.VMEM((2, scatter_rows(bins), LANES), F32),
        ]
        + exchange_semaphores(devices),
        compiler_params=pltpu.CompilerParams(
            collective_id=1, has_side_effects=True, vmem_limit_bytes=48 * 2**20
        ),
        name="collect",
    )(slot_grads, back_grads, wanted, bg_ids)


def update_kernel(
    center_y,
    params,
    adam_m,
    adam_v,
    pulls,
    new_params,
    new_m,
    new_v,
    laid,
    grads,
    held_params,
    held_m,
    held_v,
    sems,
):
    count, g_local = params.shape
    lay_out(params, laid)
    copies = []
    for hb in range(g_local // 2048):
        for half in range(2):
            block = hb * 2 + half
            rows = [feature(laid, f, block) for f in range(10)]
            made, pull_back = jax.vjp(lambda given: geometry(given, center_y), rows)
            got = [pulls[f, half, hb * 8 : hb * 8 + 8, :] for f in range(SPLAT)]

            def put(f, value):
                first = (hb * 16 + half) * 8 + f % 8
                grads[f // 8, pl.ds(first, 8, stride=16), :] = value

            given = got[:5]
            for k in range(16):
                at = 11 + 3 * k
                total = got[6] * feature(laid, at, block)
                total = total + got[7] * feature(laid, at + 1, block)
                total = total + got[8] * feature(laid, at + 2, block)
                given.append(total)
                for c in range(3):
                    put(at + c, made[5 + k] * got[6 + c])
            for f, row in enumerate(pull_back(given)[0]):
                put(f, row)
            put(10, got[5] * (1.0 - jax.nn.sigmoid(feature(laid, 10, block))))

        @pl.loop(0, 16)
        def _(chunk):
            c = hb * 16 + chunk
            columns = pl.ds(pl.multiple_of(c * LANES, LANES), LANES)
            first = pl.multiple_of(c * 8, 8)
            for group in range(-(-count // 8)):
                size = min(8, count - group * 8)
                spot = slice(group * 8, group * 8 + size)
                slope = grads[group, pl.ds(first, size), :]
                moment = 0.9 * adam_m[spot, columns] + 0.1 * slope
                power = 0.999 * adam_v[spot, columns] + 0.001 * slope * slope
                change = moment / BIAS_ONE / (jnp.sqrt(power / BIAS_TWO) + 1e-08)
                held_params[spot, columns] = params[spot, columns] - 0.05 * change
                held_m[spot, columns] = moment
                held_v[spot, columns] = power

        columns = pl.ds(hb * 2048, 2048)
        for i, (held, out) in enumerate(
            ((held_params, new_params), (held_m, new_m), (held_v, new_v))
        ):
            copies.append(
                pltpu.make_async_copy(held.at[:, columns], out.at[:, columns], sems.at[hb * 3 + i])
            )
        start(copies[-3:])
    finish(copies)


def update(params, adam_m, adam_v, pulls, center_y):
    count, g_local = params.shape
    vmem = pl.BlockSpec(memory_space=pltpu.VMEM)
    far = pl.BlockSpec(memory_space=pl.ANY)
    shape = jax.ShapeDtypeStruct(params.shape, F32)
    return pl.pallas_call(
        functools.partial(update_kernel, center_y),
        out_shape=(shape, shape, shape),
        in_specs=[vmem] * 4,
        out_specs=(far, far, far),
        scratch_shapes=[
            pltpu.VMEM((8, g_local // 16, LANES), F32),
            pltpu.VMEM((8, g_local // 16, LANES), F32),
            pltpu.VMEM((count, g_local), F32),
            pltpu.VMEM((count, g_local), F32),
            pltpu.VMEM((count, g_local), F32),
            pltpu.SemaphoreType.DMA((3 * (g_local // 2048),)),
        ],
        compiler_params=pltpu.CompilerParams(vmem_limit_bytes=48 * 2**20),
        name="update",
    )(params, adam_m, adam_v, pulls)


def per_device(
    devices,
    params,
    adam_m,
    adam_v,
    target,
    req_rows,
    tile_list,
    tile_len,
    tile_order,
    tile_pos,
    bg_ids,
):
    g_local = params.shape[1]
    tiles_here = tile_order.shape[0]
    center_y = 8.0 * (tiles_here * devices // TILES_X)
    ids = bg_ids.reshape(1, LANES)
    arrived, backs, wanted = supply(devices, params, ids, req_rows, center_y)
    slot_grads, back_grads = render_tiles(
        arrived, backs, tile_list, tile_order, tile_len, tile_pos, target
    )
    pulls = collect(devices, slot_grads, back_grads, wanted, ids, g_local)
    return update(params, adam_m, adam_v, pulls, center_y)


def solution(mesh):
    return jax.shard_map(
        functools.partial(per_device, mesh.shape["dev"]),
        mesh=mesh,
        in_specs=(
            P(None, "dev"),
            P(None, "dev"),
            P(None, "dev"),
            P(None, "dev"),
            P("dev", None),
            P("dev", None),
            P("dev"),
            P("dev", None),
            P("dev"),
            P(),
        ),
        out_specs=(P(None, "dev"), P(None, "dev"), P(None, "dev")),
        check_vma=False,
    )
```

time: 116 us -> 78.9 us (0.68)
  Pallas kernels: 107 us -> 70.7 us
    pallas_call x7 -> x3, Pallas kernels: 61.1 us -> 42.2 us  [the longest x1 21.5 us: supply(): pl.pallas_call(functools.partial(front_kernel, devices, center_y), out_sh...]
    pallas_call x1, Pallas kernels: 46.3 us -> 28.5 us  [render_tiles(): pl.pallas_call(tiles_kernel, out_shape=(jax.ShapeDtypeStruct((NEAR, 40, L...]
    unnamed x28 -> x22, local copies, waits for them, and re-layouts: 6.77 us -> 7.14 us
where the time goes in v1:
time: 78.9 us; the launch traced here: 78.5 us
  Pallas kernels  70.7 us (90%)
  local copies, waits for them, and re-layouts  7.14 us (9%)
    pallas_call x1, Pallas kernels, render_tiles(): pl.pallas_call(tiles_kernel, out_shape=(jax.ShapeDtypeStruct((NEAR, 40, L...  28.5 us
    pallas_call x1, Pallas kernels, supply(): pl.pallas_call(functools.partial(front_kernel, devices, center_y), out_sh...  21.5 us
    pallas_call x1, Pallas kernels, collect(): pl.pallas_call(functools.partial(back_kernel, devices, g_local), out_shap...  17.3 us
    unnamed x22, local copies, waits for them, and re-layouts  7.14 us
    pallas_call x1, Pallas kernels, update(): pl.pallas_call(functools.partial(update_kernel, center_y), out_shape=(sha...  3.4 us

profile of v1, /device:TPU:1, one launch (start us, length us, event | category | flops | bytes accessed | tf_op | source)
XLA Modules:
  0.0 78.5 jit_solution(2330441596443336230)
XLA Ops:
  0.6 0.0 copy-start.8
  0.6 0.6 copy-done.8
  1.3 0.0 copy-start
  1.3 1.2 %copy-done = f32[59,4096]{1,0:T(8,128)S(1)} copy-done((f32[59,4096]{1,0:T(8,128)S(1)}, f32[59,4096]{1,0:T(8,128)}, u32[]{:S(2)}) %copy-start) | copy-done | bytes 966680
  2.5 0.0 copy-start.6
  2.5 0.7 copy-done.6
  3.2 0.0 copy-start.4
  3.2 0.0 copy-start.1
  3.2 21.5 %supply.1 = (f32[10,40,128]{2,1,0:T(8,128)S(1)}, f32[8,16,128]{2,1,0:T(8,128)S(1)}, s32[1,5120]{1,0:T(1,128)S(1)}) custom-call(f32[59,4096]{1,0:T(8,128)S(1)} %copy-done, s32[1,128]{1,0:T(1,128)S(1)} %bitcast.1, s32[1,5120]{1,0:T(1,128)S(1)} %copy-done.6), custom_call_target="tpu_custom_call" | custom-call | tf_op jit(solution)/shard_map/supply/pallas_call | solution.py:346
  24.8 0.0 copy-start.9
  24.8 0.0 copy-start.10
  24.8 0.0 copy-done.4
  24.8 0.6 copy-done.9
  25.4 0.0 copy-done.10
  25.5 0.0 copy-start.5
  25.5 0.7 copy-done.5
  26.2 0.0 copy-start.7
  26.2 0.7 copy-done.7
  26.9 28.5 %render_tiles.1 = (f32[10,40,128]{2,1,0:T(8,128)S(1)}, f32[16,128]{1,0:T(8,128)S(1)}) custom-call(f32[10,40,128]{2,1,0:T(8,128)S(1)} %get-tuple-element.8.arrived, f32[8,16,128]{2,1,0:T(8,128)S(1)} %get-tuple-element.9.backs, s32[1,5120]{1,0:T(1,128)S(1)} %copy-done.4, s32[4,1280]{1,0:T(4,128)S(1)} %copy-done.5, s32[4]{0:T(128)S(1)} %copy-done.9, ...), custom_call_target="tpu_custom_call" | custom-call | tf_op jit(solution)/shard_map/render_tiles/pallas_call | solution.py:680
  55.4 17.3 %collect.1.pulls = f32[9,2,16,128]{3,2,1,0:T(8,128)S(1)} custom-call(f32[10,40,128]{2,1,0:T(8,128)S(1)} %get-tuple-element.10.grads, f32[16,128]{1,0:T(8,128)S(1)} %get-tuple-element.11.back, s32[1,5120]{1,0:T(1,128)S(1)} %get-tuple-element.12.wanted, s32[1,128]{1,0:T(1,128)S(1)} %bitcast.2), custom_call_target="tpu_custom_call" | custom-call | tf_op jit(solution)/shard_map/collect/pallas_call | solution.py:795
  72.7 0.0 copy-done.1
  72.7 0.0 copy-start.2
  72.7 1.2 %copy-done.2 = f32[59,4096]{1,0:T(8,128)S(1)} copy-done((f32[59,4096]{1,0:T(8,128)S(1)}, f32[59,4096]{1,0:T(8,128)}, u32[]{:S(2)}) %copy-start.2) | copy-done | bytes 966680
  73.9 0.0 copy-start.3
  73.9 1.2 %copy-done.3 = f32[59,4096]{1,0:T(8,128)S(1)} copy-done((f32[59,4096]{1,0:T(8,128)S(1)}, f32[59,4096]{1,0:T(8,128)}, u32[]{:S(2)}) %copy-start.3) | copy-done | bytes 966680
  75.1 3.4 %update.1 = (f32[59,4096]{1,0:T(8,128)}, f32[59,4096]{1,0:T(8,128)}, f32[59,4096]{1,0:T(8,128)}) custom-call(f32[59,4096]{1,0:T(8,128)S(1)} %copy-done.1, f32[59,4096]{1,0:T(8,128)S(1)} %copy-done.2, f32[59,4096]{1,0:T(8,128)S(1)} %copy-done.3, f32[9,2,16,128]{3,2,1,0:T(8,128)S(1)} %collect.1.pulls), custom_call_target="tpu_custom_call" | custom-call | tf_op jit(solution)/shard_map/update/pallas_call | solution.py:892
Async XLA Ops:
  0.6 0.7 copy-start.8
  1.3 1.2 %copy-start = (f32[59,4096]{1,0:T(8,128)S(1)}, f32[59,4096]{1,0:T(8,128)}, u32[]{:S(2)}) copy-start(f32[59,4096]{1,0:T(8,128)} %params.3) | copy-start | bytes 2899972
  2.5 0.7 copy-start.6
  3.2 21.6 %copy-start.4 = (s32[1,5120]{1,0:T(1,128)S(1)}, s32[1,5120]{1,0:T(1,128)}, u32[]{:S(2)}) copy-start(s32[1,5120]{1,0:T(1,128)} %tile_list.1) | copy-start | bytes 61444
  3.2 69.4 %copy-start.1 = (f32[59,4096]{1,0:T(8,128)S(1)}, f32[59,4096]{1,0:T(8,128)}, u32[]{:S(2)}) copy-start(f32[59,4096]{1,0:T(8,128)} %params.3) | copy-start | bytes 2899972
  24.8 0.7 copy-start.9
  24.8 0.7 copy-start.10
  25.5 0.7 copy-start.5
  26.2 0.7 copy-start.7
  72.7 1.2 %copy-start.2 = (f32[59,4096]{1,0:T(8,128)S(1)}, f32[59,4096]{1,0:T(8,128)}, u32[]{:S(2)}) copy-start(f32[59,4096]{1,0:T(8,128)} %adam_m.1) | copy-start | bytes 2899972
  73.9 1.2 %copy-start.3 = (f32[59,4096]{1,0:T(8,128)S(1)}, f32[59,4096]{1,0:T(8,128)}, u32[]{:S(2)}) copy-start(f32[59,4096]{1,0:T(8,128)} %adam_v.1) | copy-start | bytes 2899972

commit v2 on v1

--- a/solution.py
+++ b/solution.py
@@ -186,16 +186,11 @@
         copy.wait()
 
 
-def exchange_semaphores(devices):
-    return [
-        pltpu.SemaphoreType.DMA((NEAR,)),
-        pltpu.SemaphoreType.DMA((NEAR,)),
-        pltpu.SemaphoreType.DMA((INNER,)),
-        pltpu.SemaphoreType.DMA((INNER,)),
-        pltpu.SemaphoreType.DMA((devices // INNER,)),
-        pltpu.SemaphoreType.DMA((devices // INNER,)),
-        pltpu.SemaphoreType.DMA((3,)),
-    ]
+def sum_of(first, taken):
+    total = first
+    for k in range(1, taken.shape[0]):
+        total = total + taken[k]
+    return total
 
 
 def feature(laid, f, block):
@@ -216,159 +211,60 @@
         laid[count // 8, pl.ds(first, over), :] = params[count - over :, columns]
 
 
-def front_kernel(
-    devices,
-    center_y,
-    params,
-    bg_ids,
-    req,
-    arrived,
-    backs,
-    wanted,
-    laid,
-    splats,
-    back,
-    held,
-    part,
-    sent,
-    index,
-    ask_send,
-    ask_recv,
-    send_sem,
-    recv_sem,
-    inner_send,
-    inner_recv,
-    outer_send,
-    outer_recv,
-    local_sem,
-):
-    count, g_local = params.shape
-    chunks = g_local // LANES
-    cap = req.shape[1] // NEAR
-    greeted = greet(devices)
-    lay_out(params, laid)
-
-    def project(block):
-        rows = [feature(laid, f, block) for f in range(11)]
-        made = geometry(rows, center_y)
-        opacity = jax.nn.sigmoid(rows[10])
-        colors = []
-        for c in range(3):
-            total = made[5] * feature(laid, 11 + c, block)
-            for k in range(1, 16):
-                total = total + made[5 + k] * feature(laid, 11 + 3 * k + c, block)
-            colors.append(total + 0.5)
-        for f, row in enumerate(made[:5] + [opacity] + colors):
-            splats[f, block % 2, block // 2 * 8 : block // 2 * 8 + 8, :] = row
-
-    project(0)
-    greeted()
-    asks = []
-    for w in range(NEAR):
-        columns = pl.ds(w * cap, cap)
-        asks.append(
-            window_copy(
-                devices, w, 1, req.at[:, columns], wanted.at[:, columns], ask_send, ask_recv, local_sem.at[0]
-            )
-        )
-    start(asks)
-    for block in range(1, chunks // 8):
-        project(block)
-
-    local = wide(bg_ids[...] - lax.axis_index("dev") * g_local)
+def project(center_y, laid, splats, block):
+    rows = [feature(laid, f, block) for f in range(11)]
+    made = geometry(rows, center_y)
+    opacity = jax.nn.sigmoid(rows[10])
+    colors = []
+    for c in range(3):
+        total = made[5] * feature(laid, 11 + c, block)
+        for k in range(1, 16):
+            total = total + made[5 + k] * feature(laid, 11 + 3 * k + c, block)
+        colors.append(total + 0.5)
+    for f, row in enumerate(made[:5] + [opacity] + colors):
+        splats[f, block % 2, block // 2 * 8 : block // 2 * 8 + 8, :] = row
+
+
+def own_back(splats, mine, back):
+    local = wide(mine)
     high = jnp.right_shift(local, 7)
     low = jnp.bitwise_and(local, LANES - 1)
     eight = lax.broadcasted_iota(jnp.int32, (8, LANES), 0)
     back[...] = jnp.zeros_like(back)
     for f in range(SPLAT):
         total = jnp.zeros((8, LANES), F32)
-        for block in range(chunks // 8):
+        for block in range(2 * splats.shape[2] // 8):
             hb, half = block // 2, block % 2
             found = lane_gather(splats[f, half, hb * 8 : hb * 8 + 8, :], low)
             total = jnp.where(high == hb * 16 + 2 * eight + half, found, total)
         back[f : f + 1, :] = jnp.sum(total, axis=0, keepdims=True)
-    inner = spread(devices, INNER, inner_partner, back, held, inner_send, inner_recv)
-    start(inner)
-
-    finish(asks)
-    for r in range(wanted.shape[1] // LANES):
-        index[r : r + 1, :] = wanted[:, r * LANES : (r + 1) * LANES]
-    sends = []
-    outer = []
-    for i in reversed(range(NEAR // 2)):
-        rows = index[i * 8 : i * 8 + 8, :]
-        high = jnp.right_shift(rows, 7)
-        low = jnp.bitwise_and(rows, LANES - 1)
-
-        def pick(step, totals, high=high, low=low):
-            totals = list(totals)
-            for k in range(4):
-                for half in range(2):
-                    c = step * 4 + k
-                    here = high == 2 * c + half
-                    for f in range(SPLAT):
-                        source = wide(splats[f, half, pl.ds(c, 1), :])
-                        totals[f] = jnp.where(here, lane_gather(source, low), totals[f])
-            return tuple(totals)
-
-        none = tuple(jnp.zeros((8, LANES), F32) for _ in range(SPLAT))
-        totals = lax.fori_loop(0, chunks // 8, pick, none)
-        for half in range(2):
-            w = i * 2 + half
-            for f in range(SPLAT):
-                sent[w, f * 4 : f * 4 + 4, :] = totals[f][half * 4 : half * 4 + 4, :]
-            sent[w, 36:40, :] = jnp.zeros((4, LANES), F32)
-            sends.append(
-                window_copy(
-                    devices, w, -1, sent.at[w], arrived.at[w], send_sem, recv_sem, local_sem.at[1]
-                )
-            )
-        start(sends[-2:])
-        if i == NEAR // 2 - 2:
-            finish(inner)
-            summed = back[...]
-            for k in range(1, INNER):
-                summed = summed + held[k]
-            part[...] = summed
-            outer = spread(
-                devices, devices // INNER, outer_partner, part, backs, outer_send, outer_recv
-            )
-            start(outer)
-            backs[0] = summed
-    finish(outer)
-    finish(sends)
-
-
-def supply(devices, params, bg_ids, req_rows, center_y):
-    count, g_local = params.shape
-    slots = req_rows.shape[1]
-    vmem = pl.BlockSpec(memory_space=pltpu.VMEM)
-    return pl.pallas_call(
-        functools.partial(front_kernel, devices, center_y),
-        out_shape=(
-            jax.ShapeDtypeStruct((NEAR, 40, LANES), F32),
-            jax.ShapeDtypeStruct((devices // INNER, 16, LANES), F32),
-            jax.ShapeDtypeStruct((1, slots), jnp.int32),
-        ),
-        in_specs=[vmem] * 3,
-        out_specs=(vmem,) * 3,
-        scratch_shapes=[
-            pltpu.VMEM((8, g_local // 16, LANES), F32),
-            pltpu.VMEM((SPLAT, 2, g_local // 256, LANES), F32),
-            pltpu.VMEM((16, LANES), F32),
-            pltpu.VMEM((INNER, 16, LANES), F32),
-            pltpu.VMEM((16, LANES), F32),
-            pltpu.VMEM((NEAR, 40, LANES), F32),
-            pltpu.VMEM((slots // LANES, LANES), jnp.int32),
-            pltpu.SemaphoreType.DMA((NEAR,)),
-            pltpu.SemaphoreType.DMA((NEAR,)),
-        ]
-        + exchange_semaphores(devices),
-        compiler_params=pltpu.CompilerParams(
-            collective_id=0, has_side_effects=True, vmem_limit_bytes=48 * 2**20
-        ),
-        name="supply",
-    )(params, bg_ids, req_rows)
+
+
+def owner_gather(splats, wanted, i, sent):
+    first = i * 8 * LANES
+    rows = jnp.concatenate(
+        [wanted[:, first + r * LANES : first + (r + 1) * LANES] for r in range(8)], axis=0
+    )
+    high = jnp.right_shift(rows, 7)
+    low = jnp.bitwise_and(rows, LANES - 1)
+
+    def pick(step, totals):
+        totals = list(totals)
+        for k in range(4):
+            for half in range(2):
+                c = step * 4 + k
+                here = high == 2 * c + half
+                for f in range(SPLAT):
+                    source = wide(splats[f, half, pl.ds(c, 1), :])
+                    totals[f] = jnp.where(here, lane_gather(source, low), totals[f])
+        return tuple(totals)
+
+    none = tuple(jnp.zeros((8, LANES), F32) for _ in range(SPLAT))
+    totals = lax.fori_loop(0, splats.shape[2] // 4, pick, none)
+    for half in range(2):
+        for f in range(SPLAT):
+            sent[i * 2 + half, f * 4 : f * 4 + 4, :] = totals[f][half * 4 : half * 4 + 4, :]
+        sent[i * 2 + half, 36:40, :] = jnp.zeros((4, LANES), F32)
 
 
 def scatter_rows(bins):
@@ -418,39 +314,11 @@
         product[1] += made[:, LANES:]
 
 
-def tiles_kernel(
-    arrived,
-    backs,
-    tile_list,
-    tile_order,
-    tile_len,
-    tile_pos,
-    target,
-    slot_grads,
-    back_grads,
-    order,
-    live,
-    entries,
-    wished_in,
-    wished,
-    alphas,
-    split,
-    sums,
-    terms,
-    carried,
-    slopes,
-    color_sums,
-    entry_grads,
-    before,
-    after,
-    left,
-    right,
-    product,
+def tiles_setup(
+    tile_list, tile_order, tile_len, target, order, live, wished_in, wished, before, after
 ):
     tiles, list_len = tile_order.shape
     groups = list_len // LANES
-    lasts = groups + 1
-    back_row = tiles * groups
 
     eight = lax.broadcasted_iota(jnp.int32, (8, LANES), 0)
     lengths = jnp.zeros((8, LANES), jnp.int32)
@@ -477,33 +345,6 @@
         order[pair * 8 : pair * 8 + 8, :] = named
         live[pair * 8 : pair * 8 + 8, :] = jnp.where(ranks < lengths, 1.0, 0.0)
 
-    @pl.loop(0, back_row // 8)
-    def _(i):
-        spots = pl.ds(pl.multiple_of(i * 8, 8), 8)
-        slots = order[spots, :]
-        high = jnp.right_shift(slots, 7)
-        low = jnp.bitwise_and(slots, LANES - 1)
-
-        def window(w, totals):
-            totals = list(totals)
-            for k in range(4):
-                here = high == w * 4 + k
-                for f in range(SPLAT):
-                    source = wide(arrived[w, f * 4 + k : f * 4 + k + 1, :])
-                    totals[f] = jnp.where(here, lane_gather(source, low), totals[f])
-            return tuple(totals)
-
-        none = tuple(jnp.zeros((8, LANES), F32) for _ in range(SPLAT))
-        totals = lax.fori_loop(0, NEAR, window, none)
-        for f in range(SPLAT):
-            entries[f, spots, :] = totals[f] * live[spots, :] if f == 5 else totals[f]
-
-    summed = backs[0]
-    for k in range(1, backs.shape[0]):
-        summed = summed + backs[k]
-    for f in range(SPLAT):
-        entries[f, back_row : back_row + 1, :] = summed[f : f + 1, :]
-
     wished_in[...] = jnp.zeros_like(wished_in)
     for t in range(tiles):
         wished_in[3 * t : 3 * t + 3, :] = target[:, t * 256 : (t + 1) * 256]
@@ -517,6 +358,44 @@
     col_at = lax.broadcasted_iota(jnp.int32, (256, 256), 1)
     before[...] = jnp.where((row_at < col_at) | (col_at >= LANES), 1.0, 0.0).astype(BF16)
     after[...] = jnp.where((row_at > col_at) | (col_at >= LANES), 1.0, 0.0).astype(BF16)
+
+
+def tiles_gather(w, arrived, order, entries):
+    @pl.loop(0, order.shape[0] // 8)
+    def _(i):
+        spots = pl.ds(pl.multiple_of(i * 8, 8), 8)
+        slots = order[spots, :]
+        high = jnp.right_shift(slots, 7)
+        low = jnp.bitwise_and(slots, LANES - 1)
+        totals = [entries[f, spots, :] for f in range(SPLAT)]
+        for k in range(4):
+            here = high == w * 4 + k
+            for f in range(SPLAT):
+                source = wide(arrived[w, f * 4 + k : f * 4 + k + 1, :])
+                totals[f] = jnp.where(here, lane_gather(source, low), totals[f])
+        for f in range(SPLAT):
+            entries[f, spots, :] = totals[f]
+
+
+def tiles_render(
+    tiles,
+    tile_pos,
+    entries,
+    wished,
+    alphas,
+    split,
+    sums,
+    terms,
+    carried,
+    slopes,
+    color_sums,
+    entry_grads,
+    before,
+    after,
+):
+    lasts = alphas.shape[0]
+    groups = lasts - 1
+    back_row = tiles * groups
     entry_grads[...] = jnp.zeros_like(entry_grads)
 
     def row_of(t, j):
@@ -650,9 +529,9 @@
             for f in range(SPLAT):
                 entry_grads[row, f : f + 1, :] += made[f]
 
-    back_grads[...] = entry_grads[back_row]
-
-    @pl.loop(0, back_row)
+
+def slot_columns(order, entry_grads, left, right):
+    @pl.loop(0, order.shape[0])
     def _(r):
         column = pl.multiple_of(r * LANES, LANES)
         values = entry_grads[r]
@@ -660,7 +539,8 @@
             order[pl.ds(r, 1), :], values[0:8], values[8:9], left, right, column, 2 * NEAR
         )
 
-    scatter_product(left, right, product)
+
+def slot_values(product, slot_grads):
     for h in range(2 * NEAR):
         for half in range(2):
             eight, ninth = bin_values(product, half, h, 2 * NEAR)
@@ -671,111 +551,16 @@
         slot_grads[w, 36:40, :] = jnp.zeros((4, LANES), F32)
 
 
-def render_tiles(arrived, backs, tile_list, tile_order, tile_len, tile_pos, target):
-    tiles, list_len = tile_order.shape
-    rows = tiles * list_len // LANES
-    lasts = list_len // LANES + 1
-    vmem = pl.BlockSpec(memory_space=pltpu.VMEM)
-    smem = pl.BlockSpec(memory_space=pltpu.SMEM)
-    return pl.pallas_call(
-        tiles_kernel,
-        out_shape=(
-            jax.ShapeDtypeStruct((NEAR, 40, LANES), F32),
-            jax.ShapeDtypeStruct((16, LANES), F32),
-        ),
-        in_specs=[vmem, vmem, vmem, vmem, smem, smem, vmem],
-        out_specs=(vmem, vmem),
-        scratch_shapes=[
-            pltpu.VMEM((rows, LANES), jnp.int32),
-            pltpu.VMEM((rows, LANES), F32),
-            pltpu.VMEM((SPLAT, rows + 8, LANES), F32),
-            pltpu.VMEM((LANES, 256), F32),
-            pltpu.VMEM((tiles * 3, 256, LANES), F32),
-            pltpu.VMEM((lasts, 256, LANES), F32),
-            pltpu.VMEM((lasts, 256, 256), BF16),
-            pltpu.VMEM((lasts, 256, 256), F32),
-            pltpu.VMEM((lasts, 256, LANES), F32),
-            pltpu.VMEM((256, LANES), F32),
-            pltpu.VMEM((3, 256, LANES), F32),
-            pltpu.VMEM((3, lasts, 8, LANES), F32),
-            pltpu.VMEM((rows + 1, 16, LANES), F32),
-            pltpu.VMEM((256, 256), BF16),
-            pltpu.VMEM((256, 256), BF16),
-            pltpu.VMEM((scatter_rows(2 * NEAR), rows * LANES), BF16),
-            pltpu.VMEM((256, rows * LANES), BF16),
-            pltpu.VMEM((2, scatter_rows(2 * NEAR), LANES), F32),
-        ],
-        compiler_params=pltpu.CompilerParams(vmem_limit_bytes=48 * 2**20),
-        name="render_tiles",
-    )(arrived, backs, tile_list, tile_order, tile_len, tile_pos, target)
-
-
-def back_kernel(
-    devices,
-    g_local,
-    grads,
-    back,
-    wanted,
-    bg_ids,
-    pulls,
-    returned,
-    gathered,
-    held,
-    part,
-    left,
-    right,
-    product,
-    send_sem,
-    recv_sem,
-    inner_send,
-    inner_recv,
-    outer_send,
-    outer_recv,
-    local_sem,
-):
-    bins = g_local // 256
-    slots = wanted.shape[1]
-    greet(devices)()
-    inner = spread(devices, INNER, inner_partner, back, held, inner_send, inner_recv)
-    start(inner)
-    order = [9, 8, 7, 6, 5, 4, 3, 2, 1]
-    copies = {
-        w: window_copy(
-            devices, w, 1, grads.at[w], returned.at[w], send_sem, recv_sem, local_sem.at[0]
-        )
-        for w in order
-    }
-    start(copies.values())
-
-    def columns_of(w, source):
-        for k in range(4):
-            column = (w * 4 + k) * LANES
-            eight = source[w, pl.ds(k, 8, stride=4), :]
-            ninth = source[w, 32 + k : 33 + k, :]
-            scatter_columns(
-                wanted[:, column : column + LANES], eight, ninth, left, right, column, bins
-            )
-
-    columns_of(0, grads)
-    finish(inner)
-    summed = back[...]
-    for k in range(1, INNER):
-        summed = summed + held[k]
-    part[...] = summed
-    outer = spread(devices, devices // INNER, outer_partner, part, gathered, outer_send, outer_recv)
-    start(outer)
-    for w in reversed(order):
-        copies[w].wait()
-        columns_of(w, returned)
-    finish(outer)
-    summed = part[...]
-    for k in range(1, devices // INNER):
-        summed = summed + gathered[k]
-    mine = bg_ids[...] - lax.axis_index("dev") * g_local
-    scatter_columns(mine, summed[0:8], summed[8:9], left, right, slots, bins)
-    left[:, slots + LANES :] = jnp.zeros((left.shape[0], LANES), BF16)
-    right[:, slots + LANES :] = jnp.zeros((256, LANES), BF16)
-    scatter_product(left, right, product)
+def owner_columns(w, source, wanted, left, right, bins):
+    for k in range(4):
+        column = (w * 4 + k) * LANES
+        eight = source[w, pl.ds(k, 8, stride=4), :]
+        ninth = source[w, 32 + k : 33 + k, :]
+        index = wanted[:, column : column + LANES]
+        scatter_columns(index, eight, ninth, left, right, column, bins)
+
+
+def owner_values(product, bins, pulls):
     for hb in range(bins // 8):
         for half in range(2):
             spot = slice(hb * 8, hb * 8 + 8)
@@ -788,30 +573,291 @@
             pulls[8, half, spot, :] = ninth
 
 
-def collect(devices, slot_grads, back_grads, wanted, bg_ids, g_local):
-    depth = wanted.shape[1] + 2 * LANES
+def step_kernel(
+    devices,
+    center_y,
+    far_params,
+    far_m,
+    far_v,
+    far_target,
+    far_req,
+    far_list,
+    tile_len,
+    far_order,
+    tile_pos,
+    far_ids,
+    pulls,
+    laid,
+    params,
+    adam_m,
+    adam_v,
+    target,
+    req,
+    tile_list,
+    tile_order,
+    bg_ids,
+    splats,
+    wanted,
+    sent,
+    arrived,
+    slot_grads,
+    returned,
+    backs,
+    inner_held,
+    outer_held,
+    order,
+    live,
+    entries,
+    wished_in,
+    wished,
+    alphas,
+    split,
+    sums,
+    terms,
+    carried,
+    slopes,
+    color_sums,
+    entry_grads,
+    before,
+    after,
+    left,
+    right,
+    product,
+    owner_left,
+    owner_right,
+    owner_product,
+    load_sem,
+    local_sem,
+    ask_send,
+    ask_recv,
+    send_sem,
+    recv_sem,
+    turn_send,
+    turn_recv,
+    inner_send,
+    inner_recv,
+    outer_send,
+    outer_recv,
+):
+    g_local = params.shape[1]
     bins = g_local // 256
-    vmem = pl.BlockSpec(memory_space=pltpu.VMEM)
+    slots = req.shape[1]
+    cap = slots // NEAR
+    tiles, list_len = tile_order.shape
+    back_row = tiles * list_len // LANES
+    me = lax.axis_index("dev")
+    pairs = [
+        (far_params, params),
+        (far_req, req),
+        (far_ids, bg_ids),
+        (far_list, tile_list),
+        (far_order, tile_order),
+        (far_target, target),
+        (far_m, adam_m),
+        (far_v, adam_v),
+    ]
+    loads = [
+        pltpu.make_async_copy(given, taken, load_sem.at[i]) for i, (given, taken) in enumerate(pairs)
+    ]
+    start(loads)
+    greeted = greet(devices)
+
+    finish(loads[:3])
+    lay_out(params, laid)
+    for block in range(g_local // 1024):
+        project(center_y, laid, splats, block)
+    greeted()
+    asks = []
+    for w in range(NEAR):
+        columns = pl.ds(w * cap, cap)
+        given, taken = req.at[:, columns], wanted.at[:, columns]
+        asks.append(window_copy(devices, w, 1, given, taken, ask_send, ask_recv, local_sem.at[0]))
+    start(asks)
+    mine = bg_ids[...] - me * g_local
+    own_back(splats, mine, backs.at[0])
+
+    def spread_inner(stage):
+        return spread(
+            devices,
+            INNER,
+            inner_partner,
+            backs.at[2 * stage],
+            inner_held.at[stage],
+            inner_send.at[stage],
+            inner_recv.at[stage],
+        )
+
+    def spread_outer(stage):
+        return spread(
+            devices,
+            devices // INNER,
+            outer_partner,
+            backs.at[2 * stage + 1],
+            outer_held.at[stage],
+            outer_send.at[stage],
+            outer_recv.at[stage],
+        )
+
+    inner = spread_inner(0)
+    start(inner)
+    finish(loads[3:6])
+    tiles_setup(
+        tile_list, tile_order, tile_len, target, order, live, wished_in, wished, before, after
+    )
+    entries[...] = jnp.zeros_like(entries)
+
+    finish(asks)
+    supplies = {
+        w: window_copy(
+            devices, w, -1, sent.at[w], arrived.at[w], send_sem, recv_sem, local_sem.at[1]
+        )
+        for w in range(NEAR)
+    }
+    for i in reversed(range(NEAR // 2)):
+        owner_gather(splats, wanted, i, sent)
+        start([supplies[2 * i], supplies[2 * i + 1]])
+    finish(inner)
+    backs[1] = sum_of(backs[0], inner_held.at[0])
+    outer = spread_outer(0)
+    start(outer)
+    for w in (0, 1, 2, 9, 8, 7, 6, 5, 4, 3):
+        supplies[w].wait()
+        tiles_gather(w, arrived, order, entries)
+    entries[5, 0:back_row, :] = entries[5, 0:back_row, :] * live[...]
+    finish(outer)
+    summed = sum_of(backs[1], outer_held.at[0])
+    for f in range(SPLAT):
+        entries[f, back_row : back_row + 1, :] = summed[f : f + 1, :]
+
+    tiles_render(
+        tiles,
+        tile_pos,
+        entries,
+        wished,
+        alphas,
+        split,
+        sums,
+        terms,
+        carried,
+        slopes,
+        color_sums,
+        entry_grads,
+        before,
+        after,
+    )
+
+    backs[2] = entry_grads[back_row]
+    inner = spread_inner(1)
+    start(inner)
+    slot_columns(order, entry_grads, left, right)
+    finish(inner)
+    backs[3] = sum_of(backs[2], inner_held.at[1])
+    outer = spread_outer(1)
+    start(outer)
+    scatter_product(left, right, product)
+    slot_values(product, slot_grads)
+    turns = {
+        w: window_copy(
+            devices, w, 1, slot_grads.at[w], returned.at[w], turn_send, turn_recv, local_sem.at[2]
+        )
+        for w in range(1, NEAR)
+    }
+    start([turns[w] for w in reversed(range(1, NEAR))])
+    owner_columns(0, slot_grads, wanted, owner_left, owner_right, bins)
+    finish(outer)
+    summed = sum_of(backs[3], outer_held.at[1])
+    scatter_columns(mine, summed[0:8], summed[8:9], owner_left, owner_right, slots, bins)
+    owner_left[:, slots + LANES :] = jnp.zeros((owner_left.shape[0], LANES), BF16)
+    owner_right[:, slots + LANES :] = jnp.zeros((256, LANES), BF16)
+    for w in (1, 2, 3, 4, 9, 8, 7, 6, 5):
+        turns[w].wait()
+        owner_columns(w, returned, wanted, owner_left, owner_right, bins)
+    scatter_product(owner_left, owner_right, owner_product)
+    owner_values(owner_product, bins, pulls)
+    finish(loads[6:])
+
+
+def step(devices, center_y, *args):
+    params, adam_m, adam_v, target, req_rows, tile_list, tile_len, tile_order, tile_pos, ids = args
+    count, g_local = params.shape
+    slots = req_rows.shape[1]
+    tiles, list_len = tile_order.shape
+    rows = tiles * list_len // LANES
+    lasts = list_len // LANES + 1
+    bins = g_local // 256
+    depth = slots + 2 * LANES
+    outers = devices // INNER
+    far = pl.BlockSpec(memory_space=pltpu.HBM)
+    near = pl.BlockSpec(memory_space=pltpu.VMEM)
+    smem = pl.BlockSpec(memory_space=pltpu.SMEM)
+    dma = pltpu.SemaphoreType.DMA
+    shape = jax.ShapeDtypeStruct
+    vmem = pltpu.VMEM
     return pl.pallas_call(
-        functools.partial(back_kernel, devices, g_local),
-        out_shape=jax.ShapeDtypeStruct((SPLAT, 2, bins, LANES), F32),
-        in_specs=[vmem] * 4,
-        out_specs=vmem,
+        functools.partial(step_kernel, devices, center_y),
+        out_shape=(
+            shape((SPLAT, 2, bins, LANES), F32),
+            shape((8, g_local // 16, LANES), F32),
+            shape(params.shape, F32),
+            shape(params.shape, F32),
+            shape(params.shape, F32),
+        ),
+        in_specs=[far] * 6 + [smem, far, smem, far],
+        out_specs=(near,) * 5,
         scratch_shapes=[
-            pltpu.VMEM((NEAR, 40, LANES), F32),
-            pltpu.VMEM((devices // INNER, 16, LANES), F32),
-            pltpu.VMEM((INNER, 16, LANES), F32),
-            pltpu.VMEM((16, LANES), F32),
-            pltpu.VMEM((scatter_rows(bins), depth), BF16),
-            pltpu.VMEM((256, depth), BF16),
-            pltpu.VMEM((2, scatter_rows(bins), LANES), F32),
-        ]
-        + exchange_semaphores(devices),
+            vmem(target.shape, F32),
+            vmem(req_rows.shape, jnp.int32),
+            vmem(tile_list.shape, jnp.int32),
+            vmem(tile_order.shape, jnp.int32),
+            vmem(ids.shape, jnp.int32),
+            vmem((SPLAT, 2, g_local // 256, LANES), F32),
+            vmem(req_rows.shape, jnp.int32),
+            vmem((NEAR, 40, LANES), F32),
+            vmem((NEAR, 40, LANES), F32),
+            vmem((NEAR, 40, LANES), F32),
+            vmem((NEAR, 40, LANES), F32),
+            vmem((4, 16, LANES), F32),
+            vmem((2, INNER, 16, LANES), F32),
+            vmem((2, outers, 16, LANES), F32),
+            vmem((rows, LANES), jnp.int32),
+            vmem((rows, LANES), F32),
+            vmem((SPLAT, rows + 8, LANES), F32),
+            vmem((LANES, 256), F32),
+            vmem((tiles * 3, 256, LANES), F32),
+            vmem((lasts, 256, LANES), F32),
+            vmem((lasts, 256, 256), BF16),
+            vmem((lasts, 256, 256), F32),
+            vmem((lasts, 256, LANES), F32),
+            vmem((256, LANES), F32),
+            vmem((3, 256, LANES), F32),
+            vmem((3, lasts, 8, LANES), F32),
+            vmem((rows + 1, 16, LANES), F32),
+            vmem((256, 256), BF16),
+            vmem((256, 256), BF16),
+            vmem((scatter_rows(2 * NEAR), rows * LANES), BF16),
+            vmem((256, rows * LANES), BF16),
+            vmem((2, scatter_rows(2 * NEAR), LANES), F32),
+            vmem((scatter_rows(bins), depth), BF16),
+            vmem((256, depth), BF16),
+            vmem((2, scatter_rows(bins), LANES), F32),
+            dma((8,)),
+            dma((3,)),
+            dma((NEAR,)),
+            dma((NEAR,)),
+            dma((NEAR,)),
+            dma((NEAR,)),
+            dma((NEAR,)),
+            dma((NEAR,)),
+            dma((2, INNER)),
+            dma((2, INNER)),
+            dma((2, outers)),
+            dma((2, outers)),
+        ],
         compiler_params=pltpu.CompilerParams(
-            collective_id=1, has_side_effects=True, vmem_limit_bytes=48 * 2**20
+            collective_id=0, has_side_effects=True, vmem_limit_bytes=48 * 2**20
         ),
-        name="collect",
-    )(slot_grads, back_grads, wanted, bg_ids)
+        name="step",
+    )(*args)
 
 
 def update_kernel(
@@ -820,10 +866,10 @@
     adam_m,
     adam_v,
     pulls,
+    laid,
     new_params,
     new_m,
     new_v,
-    laid,
     grads,
     held_params,
     held_m,
@@ -831,7 +877,6 @@
     sems,
 ):
     count, g_local = params.shape
-    lay_out(params, laid)
     copies = []
     for hb in range(g_local // 2048):
         for half in range(2):
@@ -884,7 +929,7 @@
     finish(copies)
 
 
-def update(params, adam_m, adam_v, pulls, center_y):
+def update(params, adam_m, adam_v, pulls, laid, center_y):
     count, g_local = params.shape
     vmem = pl.BlockSpec(memory_space=pltpu.VMEM)
     far = pl.BlockSpec(memory_space=pl.ANY)
@@ -892,10 +937,9 @@
     return pl.pallas_call(
         functools.partial(update_kernel, center_y),
         out_shape=(shape, shape, shape),
-        in_specs=[vmem] * 4,
+        in_specs=[vmem] * 5,
         out_specs=(far, far, far),
         scratch_shapes=[
-            pltpu.VMEM((8, g_local // 16, LANES), F32),
             pltpu.VMEM((8, g_local // 16, LANES), F32),
             pltpu.VMEM((count, g_local), F32),
             pltpu.VMEM((count, g_local), F32),
@@ -904,7 +948,7 @@
         ],
         compiler_params=pltpu.CompilerParams(vmem_limit_bytes=48 * 2**20),
         name="update",
-    )(params, adam_m, adam_v, pulls)
+    )(params, adam_m, adam_v, pulls, laid)
 
 
 def per_device(
@@ -920,16 +964,22 @@
     tile_pos,
     bg_ids,
 ):
-    g_local = params.shape[1]
-    tiles_here = tile_order.shape[0]
-    center_y = 8.0 * (tiles_here * devices // TILES_X)
-    ids = bg_ids.reshape(1, LANES)
-    arrived, backs, wanted = supply(devices, params, ids, req_rows, center_y)
-    slot_grads, back_grads = render_tiles(
-        arrived, backs, tile_list, tile_order, tile_len, tile_pos, target
+    center_y = 8.0 * (tile_order.shape[0] * devices // TILES_X)
+    pulls, laid, near_params, near_m, near_v = step(
+        devices,
+        center_y,
+        params,
+        adam_m,
+        adam_v,
+        target,
+        req_rows,
+        tile_list,
+        tile_len,
+        tile_order,
+        tile_pos,
+        bg_ids.reshape(1, LANES),
     )
-    pulls = collect(devices, slot_grads, back_grads, wanted, ids, g_local)
-    return update(params, adam_m, adam_v, pulls, center_y)
+    return update(near_params, near_m, near_v, pulls, laid, center_y)
 
 
 def solution(mesh):

time: 78.9 us -> 70.3 us (0.89)
  Pallas kernels: 70.7 us -> 64.5 us
  local copies, waits for them, and re-layouts: 7.14 us -> 4.78 us
    pallas_call x3 -> x1, Pallas kernels: 67.3 us -> 61.3 us  [step(): pl.pallas_call(functools.partial(step_kernel, devices, center_y), out_sha...]
    unnamed x22 -> x16, local copies, waits for them, and re-layouts: 7.14 us -> 4.78 us
where the time goes in v2:
time: 70.3 us; the launch traced here: 69.9 us
  Pallas kernels  64.5 us (92%)
  local copies, waits for them, and re-layouts  4.78 us (7%)
    pallas_call x1, Pallas kernels, step(): pl.pallas_call(functools.partial(step_kernel, devices, center_y), out_sha...  61.3 us
    unnamed x16, local copies, waits for them, and re-layouts  4.78 us
    pallas_call x1, Pallas kernels, update(): pl.pallas_call(functools.partial(update_kernel, center_y), out_shape=(sha...  3.17 us

profile of v2, /device:TPU:1, one launch (start us, length us, event | category | flops | bytes accessed | tf_op | source)
XLA Modules:
  0.0 69.9 jit_solution(2411237750685655381)
XLA Ops:
  0.6 0.0 copy-start.7
  0.6 0.0 copy-start.6
  0.7 0.0 copy-start.5
  0.7 0.6 copy-done.7
  1.3 0.0 copy-done.6
  1.3 0.0 copy-done.5
  1.3 0.0 copy-start
  1.3 1.2 %copy-done = f32[59,4096]{1,0:T(8,128)S(1)} copy-done((f32[59,4096]{1,0:T(8,128)S(1)}, f32[59,4096]{1,0:T(8,128)}, u32[]{:S(2)}) %copy-start) | copy-done | bytes 966680
  2.5 0.0 copy-start.1
  2.5 0.7 %copy-done.1 = s32[1,5120]{1,0:T(1,128)S(1)} copy-done((s32[1,5120]{1,0:T(1,128)S(1)}, s32[1,5120]{1,0:T(1,128)}, u32[]{:S(2)}) %copy-start.1) | copy-done | bytes 20504
  3.3 0.0 copy-start.2
  3.3 0.7 %copy-done.2 = s32[1,5120]{1,0:T(1,128)S(1)} copy-done((s32[1,5120]{1,0:T(1,128)S(1)}, s32[1,5120]{1,0:T(1,128)}, u32[]{:S(2)}) %copy-start.2) | copy-done | bytes 20504
  4.0 0.0 copy-start.3
  4.0 0.7 %copy-done.3 = s32[4,1280]{1,0:T(4,128)S(1)} copy-done((s32[4,1280]{1,0:T(4,128)S(1)}, s32[4,1280]{1,0:T(4,128)}, u32[]{:S(2)}) %copy-start.3) | copy-done | bytes 20504
  4.7 0.0 copy-start.4
  4.7 0.7 %copy-done.4 = f32[3,1024]{1,0:T(4,128)S(1)} copy-done((f32[3,1024]{1,0:T(4,128)S(1)}, f32[3,1024]{1,0:T(4,128)}, u32[]{:S(2)}) %copy-start.4) | copy-done | bytes 12312
  5.4 61.3 %step.1 = (f32[9,2,16,128]{3,2,1,0:T(8,128)S(1)}, f32[8,256,128]{2,1,0:T(8,128)S(1)}, f32[59,4096]{1,0:T(8,128)S(1)}, f32[59,4096]{1,0:T(8,128)S(1)}, f32[59,4096]{1,0:T(8,128)S(1)}) custom-call(f32[59,4096]{1,0:T(8,128)S(1)} %copy-done, f32[59,4096]{1,0:T(8,128)} %far_m.1, f32[59,4096]{1,0:T(8,128)} %far_v.1, f32[3,1024]{1,0:T(4,128)S(1)} %copy-done.4, ...), custom_call_target="tpu_custom_call" | custom-call | tf_op jit(solution)/shard_map/step/pallas_call | solution.py:796
  66.7 3.2 %update.1 = (f32[59,4096]{1,0:T(8,128)}, f32[59,4096]{1,0:T(8,128)}, f32[59,4096]{1,0:T(8,128)}) custom-call(f32[59,4096]{1,0:T(8,128)S(1)} %get-tuple-element.8.params, f32[59,4096]{1,0:T(8,128)S(1)} %get-tuple-element.9.adam_m, f32[59,4096]{1,0:T(8,128)S(1)} %get-tuple-element.10.adam_v, f32[9,2,16,128]{3,2,1,0:T(8,128)S(1)} %get-tuple-element.11.pulls, ...), custom_call_target="tpu_custom_call" | custom-call | tf_op jit(solution)/shard_map/update/pallas_call | solution.py:937
Async XLA Ops:
  0.6 0.7 copy-start.7
  0.6 0.7 copy-start.6
  0.7 0.7 copy-start.5
  1.3 1.2 %copy-start = (f32[59,4096]{1,0:T(8,128)S(1)}, f32[59,4096]{1,0:T(8,128)}, u32[]{:S(2)}) copy-start(f32[59,4096]{1,0:T(8,128)} %far_params.1) | copy-start | bytes 2899972
  2.5 0.7 %copy-start.1 = (s32[1,5120]{1,0:T(1,128)S(1)}, s32[1,5120]{1,0:T(1,128)}, u32[]{:S(2)}) copy-start(s32[1,5120]{1,0:T(1,128)} %far_req.1) | copy-start | bytes 61444
  3.3 0.7 %copy-start.2 = (s32[1,5120]{1,0:T(1,128)S(1)}, s32[1,5120]{1,0:T(1,128)}, u32[]{:S(2)}) copy-start(s32[1,5120]{1,0:T(1,128)} %far_list.1) | copy-start | bytes 61444
  4.0 0.7 %copy-start.3 = (s32[4,1280]{1,0:T(4,128)S(1)}, s32[4,1280]{1,0:T(4,128)}, u32[]{:S(2)}) copy-start(s32[4,1280]{1,0:T(4,128)} %far_order.1) | copy-start | bytes 61444
  4.7 0.7 %copy-start.4 = (f32[3,1024]{1,0:T(4,128)S(1)}, f32[3,1024]{1,0:T(4,128)}, u32[]{:S(2)}) copy-start(f32[3,1024]{1,0:T(4,128)} %far_target.1) | copy-start | bytes 36868

commit v3 on v2

--- a/solution.py
+++ b/solution.py
@@ -186,6 +186,20 @@
         copy.wait()
 
 
+def receive(copies):
+    for copy in copies:
+        if copy.is_remote:
+            copy.wait_recv()
+        else:
+            copy.wait()
+
+
+def sent_off(copies):
+    for copy in copies:
+        if copy.is_remote:
+            copy.wait_send()
+
+
 def sum_of(first, taken):
     total = first
     for k in range(1, taken.shape[0]):
@@ -271,11 +285,14 @@
     return 16 * (bins + -(-bins // 8))
 
 
-def scatter_columns(index, eight, ninth, left, right, column, bins):
-    high = wide(jnp.right_shift(index, 8))
+def scatter_lanes(index, right, column):
     low = wide(jnp.bitwise_and(index, 255), 256)
     place = lax.broadcasted_iota(jnp.int32, (256, LANES), 0)
     right[:, pl.ds(column, LANES)] = jnp.where(place == low, 1.0, 0.0).astype(BF16)
+
+
+def scatter_bins(index, eight, ninth, left, column, bins):
+    high = wide(jnp.right_shift(index, 8))
 
     def put(at, here, value):
         first = value.astype(BF16).astype(F32)
@@ -418,6 +435,8 @@
 
         @pl.loop(0, lasts)
         def _(j):
+            last = jnp.maximum(j - 1, 0)
+            sums[last] = jnp.dot(split[last], before[...], preferred_element_type=F32)
             row = row_of(t, j)
             delta_x = (across + corner_x) - entry(0, row)[None]
             center_v = entry(1, row)
@@ -437,8 +456,7 @@
                 split[j, spot, :LANES] = first
                 split[j, spot, LANES:] = second
 
-        for j in range(lasts):
-            sums[j] = jnp.dot(split[j], before[...], preferred_element_type=F32)
+        sums[groups] = jnp.dot(split[groups], before[...], preferred_element_type=F32)
 
         @pl.loop(0, 8)
         def _(y):
@@ -462,6 +480,8 @@
 
         @pl.loop(0, lasts)
         def _(j):
+            last = jnp.maximum(j - 1, 0)
+            sums[last] = jnp.dot(split[last], after[...], preferred_element_type=F32)
             row = row_of(t, j)
             colors = [entry(6 + c, row)[None] for c in range(3)]
             painted = [jnp.zeros((2, 8, LANES), F32) for _ in range(3)]
@@ -480,8 +500,7 @@
             for c in range(3):
                 color_sums[c, j] = painted[c][0] + painted[c][1]
 
-        for j in range(lasts):
-            sums[j] = jnp.dot(split[j], after[...], preferred_element_type=F32)
+        sums[groups] = jnp.dot(split[groups], after[...], preferred_element_type=F32)
 
         carried[...] = jnp.zeros_like(carried)
 
@@ -535,19 +554,21 @@
     def _(r):
         column = pl.multiple_of(r * LANES, LANES)
         values = entry_grads[r]
-        scatter_columns(
-            order[pl.ds(r, 1), :], values[0:8], values[8:9], left, right, column, 2 * NEAR
-        )
-
-
-def slot_values(product, slot_grads):
-    for h in range(2 * NEAR):
+        index = order[pl.ds(r, 1), :]
+        scatter_lanes(index, right, column)
         for half in range(2):
-            eight, ninth = bin_values(product, half, h, 2 * NEAR)
+            own = index - half * NEAR * 256
+            scatter_bins(own, values[0:8], values[8:9], left.at[half], column, NEAR)
+
+
+def slot_values(product, part, slot_grads):
+    for h in range(NEAR):
+        w = part * 5 + h // 2
+        for half in range(2):
+            eight, ninth = bin_values(product, half, h, NEAR)
             for f in range(SPLAT):
                 at = f * 4 + (h % 2) * 2 + half
-                slot_grads[h // 2, at : at + 1, :] = eight[f : f + 1] if f < 8 else ninth
-    for w in range(NEAR):
+                slot_grads[w, at : at + 1, :] = eight[f : f + 1] if f < 8 else ninth
         slot_grads[w, 36:40, :] = jnp.zeros((4, LANES), F32)
 
 
@@ -557,7 +578,8 @@
         eight = source[w, pl.ds(k, 8, stride=4), :]
         ninth = source[w, 32 + k : 33 + k, :]
         index = wanted[:, column : column + LANES]
-        scatter_columns(index, eight, ninth, left, right, column, bins)
+        scatter_lanes(index, right, column)
+        scatter_bins(index, eight, ninth, left, column, bins)
 
 
 def owner_values(product, bins, pulls):
@@ -577,8 +599,6 @@
     devices,
     center_y,
     far_params,
-    far_m,
-    far_v,
     far_target,
     far_req,
     far_list,
@@ -589,8 +609,6 @@
     pulls,
     laid,
     params,
-    adam_m,
-    adam_v,
     target,
     req,
     tile_list,
@@ -653,8 +671,6 @@
         (far_list, tile_list),
         (far_order, tile_order),
         (far_target, target),
-        (far_m, adam_m),
-        (far_v, adam_v),
     ]
     loads = [
         pltpu.make_async_copy(given, taken, load_sem.at[i]) for i, (given, taken) in enumerate(pairs)
@@ -706,7 +722,7 @@
     )
     entries[...] = jnp.zeros_like(entries)
 
-    finish(asks)
+    receive(asks)
     supplies = {
         w: window_copy(
             devices, w, -1, sent.at[w], arrived.at[w], send_sem, recv_sem, local_sem.at[1]
@@ -716,15 +732,15 @@
     for i in reversed(range(NEAR // 2)):
         owner_gather(splats, wanted, i, sent)
         start([supplies[2 * i], supplies[2 * i + 1]])
-    finish(inner)
+    receive(inner)
     backs[1] = sum_of(backs[0], inner_held.at[0])
     outer = spread_outer(0)
     start(outer)
     for w in (0, 1, 2, 9, 8, 7, 6, 5, 4, 3):
-        supplies[w].wait()
+        receive([supplies[w]])
         tiles_gather(w, arrived, order, entries)
     entries[5, 0:back_row, :] = entries[5, 0:back_row, :] * live[...]
-    finish(outer)
+    receive(outer)
     summed = sum_of(backs[1], outer_held.at[0])
     for f in range(SPLAT):
         entries[f, back_row : back_row + 1, :] = summed[f : f + 1, :]
@@ -747,38 +763,41 @@
     )
 
     backs[2] = entry_grads[back_row]
+    started = asks + list(supplies.values()) + inner + outer
     inner = spread_inner(1)
     start(inner)
     slot_columns(order, entry_grads, left, right)
-    finish(inner)
+    receive(inner)
     backs[3] = sum_of(backs[2], inner_held.at[1])
     outer = spread_outer(1)
     start(outer)
-    scatter_product(left, right, product)
-    slot_values(product, slot_grads)
     turns = {
         w: window_copy(
             devices, w, 1, slot_grads.at[w], returned.at[w], turn_send, turn_recv, local_sem.at[2]
         )
         for w in range(1, NEAR)
     }
-    start([turns[w] for w in reversed(range(1, NEAR))])
+    for half in reversed(range(2)):
+        scatter_product(left.at[half], right, product)
+        slot_values(product, half, slot_grads)
+        start([turns[w] for w in reversed(range(max(1, half * 5), half * 5 + 5))])
     owner_columns(0, slot_grads, wanted, owner_left, owner_right, bins)
-    finish(outer)
+    receive(outer)
     summed = sum_of(backs[3], outer_held.at[1])
-    scatter_columns(mine, summed[0:8], summed[8:9], owner_left, owner_right, slots, bins)
+    scatter_lanes(mine, owner_right, slots)
+    scatter_bins(mine, summed[0:8], summed[8:9], owner_left, slots, bins)
     owner_left[:, slots + LANES :] = jnp.zeros((owner_left.shape[0], LANES), BF16)
     owner_right[:, slots + LANES :] = jnp.zeros((256, LANES), BF16)
     for w in (1, 2, 3, 4, 9, 8, 7, 6, 5):
-        turns[w].wait()
+        receive([turns[w]])
         owner_columns(w, returned, wanted, owner_left, owner_right, bins)
     scatter_product(owner_left, owner_right, owner_product)
     owner_values(owner_product, bins, pulls)
-    finish(loads[6:])
+    sent_off(started + inner + outer + list(turns.values()))
 
 
 def step(devices, center_y, *args):
-    params, adam_m, adam_v, target, req_rows, tile_list, tile_len, tile_order, tile_pos, ids = args
+    params, target, req_rows, tile_list, tile_len, tile_order, tile_pos, ids = args
     count, g_local = params.shape
     slots = req_rows.shape[1]
     tiles, list_len = tile_order.shape
@@ -795,16 +814,12 @@
     vmem = pltpu.VMEM
     return pl.pallas_call(
         functools.partial(step_kernel, devices, center_y),
-        out_shape=(
-            shape((SPLAT, 2, bins, LANES), F32),
-            shape((8, g_local // 16, LANES), F32),
-            shape(params.shape, F32),
-            shape(params.shape, F32),
-            shape(params.shape, F32),
-        ),
-        in_specs=[far] * 6 + [smem, far, smem, far],
-        out_specs=(near,) * 5,
+        out_shape=shape((SPLAT, 2, bins, LANES), F32),
+        in_specs=[far] * 4 + [smem, far, smem, far],
+        out_specs=near,
         scratch_shapes=[
+            vmem((8, g_local // 16, LANES), F32),
+            vmem(params.shape, F32),
             vmem(target.shape, F32),
             vmem(req_rows.shape, jnp.int32),
             vmem(tile_list.shape, jnp.int32),
@@ -834,13 +849,13 @@
             vmem((rows + 1, 16, LANES), F32),
             vmem((256, 256), BF16),
             vmem((256, 256), BF16),
-            vmem((scatter_rows(2 * NEAR), rows * LANES), BF16),
+            vmem((2, scatter_rows(NEAR), rows * LANES), BF16),
             vmem((256, rows * LANES), BF16),
-            vmem((2, scatter_rows(2 * NEAR), LANES), F32),
+            vmem((2, scatter_rows(NEAR), LANES), F32),
             vmem((scatter_rows(bins), depth), BF16),
             vmem((256, depth), BF16),
             vmem((2, scatter_rows(bins), LANES), F32),
-            dma((8,)),
+            dma((6,)),
             dma((3,)),
             dma((NEAR,)),
             dma((NEAR,)),
@@ -854,7 +869,7 @@
             dma((2, outers)),
         ],
         compiler_params=pltpu.CompilerParams(
-            collective_id=0, has_side_effects=True, vmem_limit_bytes=48 * 2**20
+            collective_id=0, has_side_effects=True, vmem_limit_bytes=60 * 2**20
         ),
         name="step",
     )(*args)
@@ -862,22 +877,34 @@
 
 def update_kernel(
     center_y,
+    far_params,
+    far_m,
+    far_v,
+    far_pulls,
+    new_params,
+    new_m,
+    new_v,
     params,
     adam_m,
     adam_v,
     pulls,
     laid,
-    new_params,
-    new_m,
-    new_v,
     grads,
     held_params,
     held_m,
     held_v,
+    load_sem,
     sems,
 ):
     count, g_local = params.shape
+    pairs = [(far_params, params), (far_pulls, pulls), (far_m, adam_m), (far_v, adam_v)]
+    loads = [
+        pltpu.make_async_copy(given, taken, load_sem.at[i]) for i, (given, taken) in enumerate(pairs)
+    ]
+    start(loads)
     copies = []
+    finish(loads[:2])
+    lay_out(params, laid)
     for hb in range(g_local // 2048):
         for half in range(2):
             block = hb * 2 + half
@@ -901,6 +928,9 @@
             for f, row in enumerate(pull_back(given)[0]):
                 put(f, row)
             put(10, got[5] * (1.0 - jax.nn.sigmoid(feature(laid, 10, block))))
+
+        if hb == 0:
+            finish(loads[2:])
 
         @pl.loop(0, 16)
         def _(chunk):
@@ -929,26 +959,31 @@
     finish(copies)
 
 
-def update(params, adam_m, adam_v, pulls, laid, center_y):
+def update(params, adam_m, adam_v, pulls, center_y):
     count, g_local = params.shape
-    vmem = pl.BlockSpec(memory_space=pltpu.VMEM)
-    far = pl.BlockSpec(memory_space=pl.ANY)
+    far = pl.BlockSpec(memory_space=pltpu.HBM)
     shape = jax.ShapeDtypeStruct(params.shape, F32)
     return pl.pallas_call(
         functools.partial(update_kernel, center_y),
         out_shape=(shape, shape, shape),
-        in_specs=[vmem] * 5,
+        in_specs=[far] * 4,
         out_specs=(far, far, far),
         scratch_shapes=[
+            pltpu.VMEM((count, g_local), F32),
+            pltpu.VMEM((count, g_local), F32),
+            pltpu.VMEM((count, g_local), F32),
+            pltpu.VMEM(pulls.shape, F32),
+            pltpu.VMEM((8, g_local // 16, LANES), F32),
             pltpu.VMEM((8, g_local // 16, LANES), F32),
             pltpu.VMEM((count, g_local), F32),
             pltpu.VMEM((count, g_local), F32),
             pltpu.VMEM((count, g_local), F32),
+            pltpu.SemaphoreType.DMA((4,)),
             pltpu.SemaphoreType.DMA((3 * (g_local // 2048),)),
         ],
-        compiler_params=pltpu.CompilerParams(vmem_limit_bytes=48 * 2**20),
+        compiler_params=pltpu.CompilerParams(vmem_limit_bytes=60 * 2**20),
         name="update",
-    )(params, adam_m, adam_v, pulls, laid)
+    )(params, adam_m, adam_v, pulls)
 
 
 def per_device(
@@ -965,12 +1000,10 @@
     bg_ids,
 ):
     center_y = 8.0 * (tile_order.shape[0] * devices // TILES_X)
-    pulls, laid, near_params, near_m, near_v = step(
+    pulls = step(
         devices,
         center_y,
         params,
-        adam_m,
-        adam_v,
         target,
         req_rows,
         tile_list,
@@ -979,7 +1012,7 @@
         tile_pos,
         bg_ids.reshape(1, LANES),
     )
-    return update(near_params, near_m, near_v, pulls, laid, center_y)
+    return update(params, adam_m, adam_v, pulls, center_y)
 
 
 def solution(mesh):

time: 70.3 us -> 74.5 us (1.060)
  Pallas kernels: 64.5 us -> 73.7 us
  local copies, waits for them, and re-layouts: 4.78 us -> 0 us
    pallas_call x1, Pallas kernels: 61.3 us -> 69 us  [step(): pl.pallas_call(functools.partial(step_kernel, devices, center_y), out_sha...]
    unnamed x16 -> x0, local copies, waits for them, and re-layouts: 4.78 us -> none
    pallas_call x1, Pallas kernels: 3.17 us -> 4.74 us  [update(): pl.pallas_call(functools.partial(update_kernel, center_y), out_shape=(sha...]
where the time goes in v3:
time: 74.5 us; the launch traced here: 74.4 us
  Pallas kernels  73.7 us (99%)
    pallas_call x1, Pallas kernels, step(): pl.pallas_call(functools.partial(step_kernel, devices, center_y), out_sha...  69 us
    pallas_call x1, Pallas kernels, update(): pl.pallas_call(functools.partial(update_kernel, center_y), out_shape=(sha...  4.74 us

profile of v3, /device:TPU:1, one launch (start us, length us, event | category | flops | bytes accessed | tf_op | source)
XLA Modules:
  0.0 74.4 jit_solution(12709222367004278772)
XLA Ops:
  0.6 69.0 %step.1.far_pulls = f32[9,2,16,128]{3,2,1,0:T(8,128)} custom-call(f32[59,4096]{1,0:T(8,128)} %far_params.3, f32[3,1024]{1,0:T(4,128)} %far_target.1, s32[1,5120]{1,0:T(1,128)} %far_req.1, s32[1,5120]{1,0:T(1,128)} %far_list.1, s32[4]{0:T(128)} %tile_len.1, s32[4,1280]{1,0:T(4,128)} %far_order.1, s32[4]{0:T(128)} %tile_pos.1, s32[1,128]{1,0:T(1,128)} %bitcast.1), custom_call_target="tpu_custom_call" | custom-call | tf_op jit(solution)/shard_map/step/pallas_call | solution.py:815
  69.6 4.7 %update.1 = (f32[59,4096]{1,0:T(8,128)}, f32[59,4096]{1,0:T(8,128)}, f32[59,4096]{1,0:T(8,128)}) custom-call(f32[59,4096]{1,0:T(8,128)} %far_params.3, f32[59,4096]{1,0:T(8,128)} %far_m.1, f32[59,4096]{1,0:T(8,128)} %far_v.1, f32[9,2,16,128]{3,2,1,0:T(8,128)} %step.1.far_pulls), custom_call_target="tpu_custom_call" | custom-call | tf_op jit(solution)/shard_map/update/pallas_call | solution.py:966

commit v4 on v3

--- a/solution.py
+++ b/solution.py
@@ -313,22 +313,25 @@
     return eight, product[half, at : at + 1, :] + product[half, at + 8 : at + 9, :]
 
 
+def add_product(left, right, first, depth, product):
+    columns = pl.ds(first, depth)
+    made = lax.dot_general(
+        left[:, columns],
+        right[:, columns],
+        (((1,), (1,)), ((), ())),
+        preferred_element_type=F32,
+    )
+    product[0] += made[:, :LANES]
+    product[1] += made[:, LANES:]
+
+
 def scatter_product(left, right, product):
-    depth = left.shape[1]
-    step = 768 if depth % 768 == 0 else 1280
+    step = 1280
     product[...] = jnp.zeros_like(product)
 
-    @pl.loop(0, depth // step)
+    @pl.loop(0, left.shape[1] // step)
     def _(i):
-        columns = pl.ds(pl.multiple_of(i * step, LANES), step)
-        made = lax.dot_general(
-            left[:, columns],
-            right[:, columns],
-            (((1,), (1,)), ((), ())),
-            preferred_element_type=F32,
-        )
-        product[0] += made[:, :LANES]
-        product[1] += made[:, LANES:]
+        add_product(left, right, pl.multiple_of(i * step, LANES), step, product)
 
 
 def tiles_setup(
@@ -435,8 +438,6 @@
 
         @pl.loop(0, lasts)
         def _(j):
-            last = jnp.maximum(j - 1, 0)
-            sums[last] = jnp.dot(split[last], before[...], preferred_element_type=F32)
             row = row_of(t, j)
             delta_x = (across + corner_x) - entry(0, row)[None]
             center_v = entry(1, row)
@@ -456,7 +457,8 @@
                 split[j, spot, :LANES] = first
                 split[j, spot, LANES:] = second
 
-        sums[groups] = jnp.dot(split[groups], before[...], preferred_element_type=F32)
+        for j in range(lasts):
+            sums[j] = jnp.dot(split[j], before[...], preferred_element_type=F32)
 
         @pl.loop(0, 8)
         def _(y):
@@ -480,8 +482,6 @@
 
         @pl.loop(0, lasts)
         def _(j):
-            last = jnp.maximum(j - 1, 0)
-            sums[last] = jnp.dot(split[last], after[...], preferred_element_type=F32)
             row = row_of(t, j)
             colors = [entry(6 + c, row)[None] for c in range(3)]
             painted = [jnp.zeros((2, 8, LANES), F32) for _ in range(3)]
@@ -500,7 +500,8 @@
             for c in range(3):
                 color_sums[c, j] = painted[c][0] + painted[c][1]
 
-        sums[groups] = jnp.dot(split[groups], after[...], preferred_element_type=F32)
+        for j in range(lasts):
+            sums[j] = jnp.dot(split[j], after[...], preferred_element_type=F32)
 
         carried[...] = jnp.zeros_like(carried)
 
@@ -722,21 +723,27 @@
     )
     entries[...] = jnp.zeros_like(entries)
 
-    receive(asks)
     supplies = {
         w: window_copy(
             devices, w, -1, sent.at[w], arrived.at[w], send_sem, recv_sem, local_sem.at[1]
         )
         for w in range(NEAR)
     }
-    for i in reversed(range(NEAR // 2)):
+
+    def answer(i):
+        receive(asks[2 * i : 2 * i + 2])
         owner_gather(splats, wanted, i, sent)
         start([supplies[2 * i], supplies[2 * i + 1]])
+
+    answer(0)
+    answer(1)
     receive(inner)
     backs[1] = sum_of(backs[0], inner_held.at[0])
     outer = spread_outer(0)
     start(outer)
-    for w in (0, 1, 2, 9, 8, 7, 6, 5, 4, 3):
+    for i in (4, 3, 2):
+        answer(i)
+    for w in (0, 1, 2, 3, 5, 4, 7, 6, 9, 8):
         receive([supplies[w]])
         tiles_gather(w, arrived, order, entries)
     entries[5, 0:back_row, :] = entries[5, 0:back_row, :] * live[...]
@@ -767,10 +774,6 @@
     inner = spread_inner(1)
     start(inner)
     slot_columns(order, entry_grads, left, right)
-    receive(inner)
-    backs[3] = sum_of(backs[2], inner_held.at[1])
-    outer = spread_outer(1)
-    start(outer)
     turns = {
         w: window_copy(
             devices, w, 1, slot_grads.at[w], returned.at[w], turn_send, turn_recv, local_sem.at[2]
@@ -781,17 +784,24 @@
         scatter_product(left.at[half], right, product)
         slot_values(product, half, slot_grads)
         start([turns[w] for w in reversed(range(max(1, half * 5), half * 5 + 5))])
+        if half == 1:
+            receive(inner)
+            backs[3] = sum_of(backs[2], inner_held.at[1])
+            outer = spread_outer(1)
+            start(outer)
+    owner_product[...] = jnp.zeros_like(owner_product)
     owner_columns(0, slot_grads, wanted, owner_left, owner_right, bins)
-    receive(outer)
-    summed = sum_of(backs[3], outer_held.at[1])
-    scatter_lanes(mine, owner_right, slots)
-    scatter_bins(mine, summed[0:8], summed[8:9], owner_left, slots, bins)
-    owner_left[:, slots + LANES :] = jnp.zeros((owner_left.shape[0], LANES), BF16)
-    owner_right[:, slots + LANES :] = jnp.zeros((256, LANES), BF16)
-    for w in (1, 2, 3, 4, 9, 8, 7, 6, 5):
+    add_product(owner_left, owner_right, 0, cap, owner_product)
+    for w in (5, 1, 2, 3, 4, 7, 6, 9, 8):
         receive([turns[w]])
         owner_columns(w, returned, wanted, owner_left, owner_right, bins)
-    scatter_product(owner_left, owner_right, owner_product)
+        add_product(owner_left, owner_right, w * cap, cap, owner_product)
+        if w == 4:
+            receive(outer)
+            summed = sum_of(backs[3], outer_held.at[1])
+            scatter_lanes(mine, owner_right, slots)
+            scatter_bins(mine, summed[0:8], summed[8:9], owner_left, slots, bins)
+            add_product(owner_left, owner_right, slots, LANES, owner_product)
     owner_values(owner_product, bins, pulls)
     sent_off(started + inner + outer + list(turns.values()))
 
@@ -804,7 +814,7 @@
     rows = tiles * list_len // LANES
     lasts = list_len // LANES + 1
     bins = g_local // 256
-    depth = slots + 2 * LANES
+    depth = slots + LANES
     outers = devices // INNER
     far = pl.BlockSpec(memory_space=pltpu.HBM)
     near = pl.BlockSpec(memory_space=pltpu.VMEM)

time: 74.5 us -> 62.7 us (0.84)
  Pallas kernels: 73.7 us -> 61.8 us
    pallas_call x1, Pallas kernels: 69 us -> 57.1 us  [step(): pl.pallas_call(functools.partial(step_kernel, devices, center_y), out_sha...]
where the time goes in v4:
time: 62.7 us; the launch traced here: 62.5 us
  Pallas kernels  61.8 us (99%)
  between operations  0.64 us (1%)
    pallas_call x1, Pallas kernels, step(): pl.pallas_call(functools.partial(step_kernel, devices, center_y), out_sha...  57.1 us
    pallas_call x1, Pallas kernels, update(): pl.pallas_call(functools.partial(update_kernel, center_y), out_shape=(sha...  4.74 us

profile of v4, /device:TPU:1, one launch (start us, length us, event | category | flops | bytes accessed | tf_op | source)
XLA Modules:
  0.0 62.5 jit_solution(12652619139955710511)
XLA Ops:
  0.6 57.1 %step.1.far_pulls = f32[9,2,16,128]{3,2,1,0:T(8,128)} custom-call(f32[59,4096]{1,0:T(8,128)} %far_params.3, f32[3,1024]{1,0:T(4,128)} %far_target.1, s32[1,5120]{1,0:T(1,128)} %far_req.1, s32[1,5120]{1,0:T(1,128)} %far_list.1, s32[4]{0:T(128)} %tile_len.1, s32[4,1280]{1,0:T(4,128)} %far_order.1, s32[4]{0:T(128)} %tile_pos.1, s32[1,128]{1,0:T(1,128)} %bitcast.1), custom_call_target="tpu_custom_call" | custom-call | tf_op jit(solution)/shard_map/step/pallas_call | solution.py:825
  57.7 4.7 %update.1 = (f32[59,4096]{1,0:T(8,128)}, f32[59,4096]{1,0:T(8,128)}, f32[59,4096]{1,0:T(8,128)}) custom-call(f32[59,4096]{1,0:T(8,128)} %far_params.3, f32[59,4096]{1,0:T(8,128)} %far_m.1, f32[59,4096]{1,0:T(8,128)} %far_v.1, f32[9,2,16,128]{3,2,1,0:T(8,128)} %step.1.far_pulls), custom_call_target="tpu_custom_call" | custom-call | tf_op jit(solution)/shard_map/update/pallas_call | solution.py:976

commit v5 on v4

--- a/solution.py
+++ b/solution.py
@@ -212,10 +212,10 @@
     return laid[f // 8, pl.ds(first, 8, stride=16), :]
 
 
-def lay_out(params, laid):
-    count, g_local = params.shape
-
-    @pl.loop(0, g_local // LANES)
+def lay_out(params, laid, first_chunk, last_chunk):
+    count = params.shape[0]
+
+    @pl.loop(first_chunk, last_chunk)
     def _(c):
         columns = pl.ds(pl.multiple_of(c * LANES, LANES), LANES)
         first = pl.multiple_of(c * 8, 8)
@@ -326,12 +326,8 @@
 
 
 def scatter_product(left, right, product):
-    step = 1280
     product[...] = jnp.zeros_like(product)
-
-    @pl.loop(0, left.shape[1] // step)
-    def _(i):
-        add_product(left, right, pl.multiple_of(i * step, LANES), step, product)
+    add_product(left, right, 0, left.shape[1], product)
 
 
 def tiles_setup(
@@ -381,9 +377,8 @@
 
 
 def tiles_gather(w, arrived, order, entries):
-    @pl.loop(0, order.shape[0] // 8)
-    def _(i):
-        spots = pl.ds(pl.multiple_of(i * 8, 8), 8)
+    for i in range(order.shape[0] // 8):
+        spots = pl.ds(i * 8, 8)
         slots = order[spots, :]
         high = jnp.right_shift(slots, 7)
         low = jnp.bitwise_and(slots, LANES - 1)
@@ -460,11 +455,11 @@
         for j in range(lasts):
             sums[j] = jnp.dot(split[j], before[...], preferred_element_type=F32)
 
-        @pl.loop(0, 8)
+        @pl.loop(0, 4)
         def _(y):
-            spot = pl.ds(pl.multiple_of(y * 32, 32), 32)
-            gone = jnp.zeros((32, LANES), F32)
-            seen = [jnp.zeros((4, 8, LANES), F32) for _ in range(3)]
+            spot = pl.ds(pl.multiple_of(y * 64, 64), 64)
+            gone = jnp.zeros((64, LANES), F32)
+            seen = [jnp.zeros((8, 8, LANES), F32) for _ in range(3)]
             for j in range(lasts):
                 row = row_of(t, j)
                 transmit = jnp.exp(gone + sums[j, spot, :LANES])
@@ -472,9 +467,9 @@
                 weight = alphas[j, spot, :] * transmit
                 terms[j, spot, :] = weight
                 for c in range(3):
-                    seen[c] = seen[c] + weight.reshape(4, 8, LANES) * entry(6 + c, row)[None]
+                    seen[c] = seen[c] + weight.reshape(8, 8, LANES) * entry(6 + c, row)[None]
             for c in range(3):
-                slopes[c, spot, :] = seen[c].reshape(32, LANES)
+                slopes[c, spot, :] = seen[c].reshape(64, LANES)
 
         for c in range(3):
             color = jnp.sum(slopes[c], axis=1, keepdims=True)
@@ -680,7 +675,7 @@
     greeted = greet(devices)
 
     finish(loads[:3])
-    lay_out(params, laid)
+    lay_out(params, laid, 0, g_local // LANES)
     for block in range(g_local // 1024):
         project(center_y, laid, splats, block)
     greeted()
@@ -907,15 +902,18 @@
     sems,
 ):
     count, g_local = params.shape
-    pairs = [(far_params, params), (far_pulls, pulls), (far_m, adam_m), (far_v, adam_v)]
-    loads = [
-        pltpu.make_async_copy(given, taken, load_sem.at[i]) for i, (given, taken) in enumerate(pairs)
-    ]
+    loads = [pltpu.make_async_copy(far_pulls, pulls, load_sem.at[0])]
+    for hb in range(g_local // 2048):
+        columns = pl.ds(hb * 2048, 2048)
+        for given, taken in ((far_params, params), (far_m, adam_m), (far_v, adam_v)):
+            given, taken = given.at[:, columns], taken.at[:, columns]
+            loads.append(pltpu.make_async_copy(given, taken, load_sem.at[len(loads)]))
     start(loads)
     copies = []
-    finish(loads[:2])
-    lay_out(params, laid)
+    finish(loads[:1])
     for hb in range(g_local // 2048):
+        finish(loads[1 + 3 * hb : 2 + 3 * hb])
+        lay_out(params, laid, hb * 16, hb * 16 + 16)
         for half in range(2):
             block = hb * 2 + half
             rows = [feature(laid, f, block) for f in range(10)]
@@ -939,8 +937,7 @@
                 put(f, row)
             put(10, got[5] * (1.0 - jax.nn.sigmoid(feature(laid, 10, block))))
 
-        if hb == 0:
-            finish(loads[2:])
+        finish(loads[2 + 3 * hb : 4 + 3 * hb])
 
         @pl.loop(0, 16)
         def _(chunk):
@@ -988,7 +985,7 @@
             pltpu.VMEM((count, g_local), F32),
             pltpu.VMEM((count, g_local), F32),
             pltpu.VMEM((count, g_local), F32),
-            pltpu.SemaphoreType.DMA((4,)),
+            pltpu.SemaphoreType.DMA((1 + 3 * (g_local // 2048),)),
             pltpu.SemaphoreType.DMA((3 * (g_local // 2048),)),
         ],
         compiler_params=pltpu.CompilerParams(vmem_limit_bytes=60 * 2**20),

time: 62.7 us -> 60.6 us (0.967)
  Pallas kernels: 61.8 us -> 59.8 us
    pallas_call x1, Pallas kernels: 57.1 us -> 55.2 us  [step(): pl.pallas_call(functools.partial(step_kernel, devices, center_y), out_sha...]
where the time goes in v5:
time: 60.6 us; the launch traced here: 60.4 us
  Pallas kernels  59.8 us (99%)
  between operations  0.64 us (1%)
    pallas_call x1, Pallas kernels, step(): pl.pallas_call(functools.partial(step_kernel, devices, center_y), out_sha...  55.2 us
    pallas_call x1, Pallas kernels, update(): pl.pallas_call(functools.partial(update_kernel, center_y), out_shape=(sha...  4.58 us

profile of v5, /device:TPU:1, one launch (start us, length us, event | category | flops | bytes accessed | tf_op | source)
XLA Modules:
  0.0 60.4 jit_solution(9217759908646848063)
XLA Ops:
  0.6 55.2 %step.1.far_pulls = f32[9,2,16,128]{3,2,1,0:T(8,128)} custom-call(f32[59,4096]{1,0:T(8,128)} %far_params.3, f32[3,1024]{1,0:T(4,128)} %far_target.1, s32[1,5120]{1,0:T(1,128)} %far_req.1, s32[1,5120]{1,0:T(1,128)} %far_list.1, s32[4]{0:T(128)} %tile_len.1, s32[4,1280]{1,0:T(4,128)} %far_order.1, s32[4]{0:T(128)} %tile_pos.1, s32[1,128]{1,0:T(1,128)} %bitcast.1), custom_call_target="tpu_custom_call" | custom-call | tf_op jit(solution)/shard_map/step/pallas_call | solution.py:820
  55.9 4.6 %update.1 = (f32[59,4096]{1,0:T(8,128)}, f32[59,4096]{1,0:T(8,128)}, f32[59,4096]{1,0:T(8,128)}) custom-call(f32[59,4096]{1,0:T(8,128)} %far_params.3, f32[59,4096]{1,0:T(8,128)} %far_m.1, f32[59,4096]{1,0:T(8,128)} %far_v.1, f32[9,2,16,128]{3,2,1,0:T(8,128)} %step.1.far_pulls), custom_call_target="tpu_custom_call" | custom-call | tf_op jit(solution)/shard_map/update/pallas_call | solution.py:973

commit v6 on v5

--- a/solution.py
+++ b/solution.py
@@ -273,8 +273,9 @@
                     totals[f] = jnp.where(here, lane_gather(source, low), totals[f])
         return tuple(totals)
 
-    none = tuple(jnp.zeros((8, LANES), F32) for _ in range(SPLAT))
-    totals = lax.fori_loop(0, splats.shape[2] // 4, pick, none)
+    totals = tuple(jnp.zeros((8, LANES), F32) for _ in range(SPLAT))
+    for step in range(splats.shape[2] // 4):
+        totals = pick(step, totals)
     for half in range(2):
         for f in range(SPLAT):
             sent[i * 2 + half, f * 4 : f * 4 + 4, :] = totals[f][half * 4 : half * 4 + 4, :]

time: 60.6 us -> 60.4 us (level)
  no operation moved by 1% of the time
where the time goes in v6:
time: 60.4 us; the launch traced here: 60.3 us
  Pallas kernels  59.6 us (99%)
  between operations  0.64 us (1%)
    pallas_call x1, Pallas kernels, step(): pl.pallas_call(functools.partial(step_kernel, devices, center_y), out_sha...  55 us
    pallas_call x1, Pallas kernels, update(): pl.pallas_call(functools.partial(update_kernel, center_y), out_shape=(sha...  4.58 us

profile of v6, /device:TPU:1, one launch (start us, length us, event | category | flops | bytes accessed | tf_op | source)
XLA Modules:
  0.0 60.3 jit_solution(15792198481999259435)
XLA Ops:
  0.6 55.0 %step.1.far_pulls = f32[9,2,16,128]{3,2,1,0:T(8,128)} custom-call(f32[59,4096]{1,0:T(8,128)} %far_params.3, f32[3,1024]{1,0:T(4,128)} %far_target.1, s32[1,5120]{1,0:T(1,128)} %far_req.1, s32[1,5120]{1,0:T(1,128)} %far_list.1, s32[4]{0:T(128)} %tile_len.1, s32[4,1280]{1,0:T(4,128)} %far_order.1, s32[4]{0:T(128)} %tile_pos.1, s32[1,128]{1,0:T(1,128)} %bitcast.1), custom_call_target="tpu_custom_call" | custom-call | tf_op jit(solution)/shard_map/step/pallas_call | solution.py:821
  55.7 4.6 %update.1 = (f32[59,4096]{1,0:T(8,128)}, f32[59,4096]{1,0:T(8,128)}, f32[59,4096]{1,0:T(8,128)}) custom-call(f32[59,4096]{1,0:T(8,128)} %far_params.3, f32[59,4096]{1,0:T(8,128)} %far_m.1, f32[59,4096]{1,0:T(8,128)} %far_v.1, f32[9,2,16,128]{3,2,1,0:T(8,128)} %step.1.far_pulls), custom_call_target="tpu_custom_call" | custom-call | tf_op jit(solution)/shard_map/update/pallas_call | solution.py:974
